TPU v7x, 32 devices: a whole 2x2x4 slice. The times are simulated.
32 devices in a mesh: band: 4 (over y, x), tok: 8 (over z, core).
Axes of the slice: x: 2, y: 2, z: 4, core: 2. Of those that a mesh axis runs over, the one named last changes fastest.
Arguments:
- pixels: bfloat16 [4, 8, 1024, 768], P(None, 'tok', None, 'band'), may hold values from -6 to 6
- wavelengths: float32 [32], replicated, may hold values from 0.4 to 2.5
- wave_index: int32 [7, 12], replicated, may hold values from 0 to 31
- band_counts: int32 [7], replicated, may hold values from 1 to 12, as said below
- sensors: int32 [4, 8, 4], P(None, 'tok'), may hold values from 0 to 6
- chip_lengths: int32 [4, 8, 4], P(None, 'tok'), may hold values from 0 to 1024, as said below
- meta_rows: bfloat16 [4, 8, 4, 768], P('band', 'tok'), may hold values from -6 to 6
- w_qkv: bfloat16 [768, 2304], P(('band', 'tok')), may hold values from -0.21875 to 0.21875
- w_out: bfloat16 [768, 768], P(('band', 'tok')), may hold values from -0.875 to 0.875
- w_up: bfloat16 [768, 3072], P(('band', 'tok')), may hold values from -0.21875 to 0.21875
- b_up: bfloat16 [3072], P(('band', 'tok')), may hold values from -3 to 3
- w_down: bfloat16 [3072, 768], P(('band', 'tok')), may hold values from -0.109375 to 0.109375
- norm_gains: bfloat16 [2, 768], P(None, ('band', 'tok')), may hold values from 0.5 to 1.5
- shifts: bfloat16 [4, 768], P(None, ('band', 'tok')), may hold values from -3 to 3
- gen_qkv: float32 [128, 384], replicated, may hold values from -0.5 to 0.5
- gen_out: float32 [128, 128], replicated, may hold values from -0.5 to 0.5
- gen_ff1: float32 [128, 2048], replicated, may hold values from -0.5 to 0.5
- gen_ff2: float32 [2048, 128], replicated, may hold values from -0.125 to 0.125
- gen_gains: float32 [2, 128], replicated, may hold values from 0.5 to 1.5
- gen_shifts: float32 [2, 128], replicated, may hold values from -2 to 2
- latent_tokens: float32 [128, 128], replicated, may hold values from -6 to 6
- bias_token: float32 [128], replicated, may hold values from -6 to 6
- fc_kernel: float32 [128, 49152], P(None, 'tok'), may hold values from -0.0234375 to 0.0234375
- fc_bias: float32 [128, 768], replicated, may hold values from -0.25 to 0.25
- d_out: bfloat16 [4, 8, 1032, 768], P('band', 'tok'), may hold values from -6 to 6
Outputs:
- out: float32 [4, 8, 1032, 768], P('band', 'tok')
- d_pixels: float32 [4, 8, 1024, 768], P(None, 'tok', None, 'band')
- d_meta: float32 [4, 8, 4, 768], P('band', 'tok')
- d_w_qkv: float32 [768, 2304], P(('band', 'tok'))
- d_w_out: float32 [768, 768], P(('band', 'tok'))
- d_w_up: float32 [768, 3072], P(('band', 'tok'))
- d_b_up: float32 [3072], P(('band', 'tok'))
- d_w_down: float32 [3072, 768], P(('band', 'tok'))
- d_norm_gains: float32 [2, 768], P(None, ('band', 'tok'))
- d_shifts: float32 [4, 768], P(None, ('band', 'tok'))
- d_gen_qkv: float32 [128, 384], replicated
- d_gen_out: float32 [128, 128], replicated
- d_gen_ff1: float32 [128, 2048], replicated
- d_gen_ff2: float32 [2048, 128], replicated
- d_gen_gains: float32 [2, 128], replicated
- d_gen_shifts: float32 [2, 128], replicated
- d_latent: float32 [128, 128], replicated
- d_bias_token: float32 [128], replicated
- d_fc_kernel: float32 [128, 49152], P(None, 'tok')
- d_fc_bias: float32 [128, 768], replicated
Inputs may be any that keep to these rules, and one draw needn't show every extreme that they name: `band_counts`: some sensor uses all 12 band slots. `chip_lengths`: each frame holds either one chip of 1024 patches in slot 0 with zeros in the other slots, or 4 chips of 256 patches; both kinds occur.
All inputs are finite; a program needn't handle non-finite values.
Results may differ from a plain program's by a relative error of at most 0.019.
Values may be sent and summed in bfloat16 or wider, within the bound.
No kernel may reach another device: no remote copies, remote signals or barrier semaphores. Data moves between devices by JAX's collectives and lax.ppermute only.
A program may use at most 256 MiB of HBM per device.

v0:
```python
import math

import jax
import jax.numpy as jnp
from jax import lax
from jax.sharding import PartitionSpec as P

D = 768
HEADS = 12
HD = 64
FF = 3072
WG = 128
GHEADS = 4
GHD = 32
NLAT = 128
PIX = 64
SENSORS = 7
BMAX = 12
CHIP = 256
CAP = 4
FRAME = 1024
ROWS = 1032


exact_precision = lax.Precision.HIGHEST
norm_epsilon = 1e-05
masked_score = -1000000000.0


def layer_norm(values, gain_row, shift_row):
    average = jnp.mean(values, axis=-1, keepdims=True)
    centered = values - average
    variance = jnp.mean(centered * centered, axis=-1, keepdims=True)
    return centered * lax.rsqrt(variance + norm_epsilon) * gain_row + shift_row


def norm_forward(values, gain_row, shift_row):
    average = jnp.mean(values, axis=-1, keepdims=True)
    centered = values - average
    variance = jnp.mean(centered * centered, axis=-1, keepdims=True)
    inv_scale = lax.rsqrt(variance + norm_epsilon)
    normalized = centered * inv_scale
    return (normalized * gain_row + shift_row, normalized, inv_scale)


def norm_backward(grad_rows, normalized, inv_scale, gain_row):
    scaled = grad_rows * gain_row
    grad_in = inv_scale * (
        scaled
        - jnp.mean(scaled, axis=-1, keepdims=True)
        - normalized * jnp.mean(scaled * normalized, axis=-1, keepdims=True)
    )
    return (grad_in, jnp.sum(grad_rows * normalized, axis=0), jnp.sum(grad_rows, axis=0))


def contract_rows(left, right):
    return lax.dot_general(
        left, right, (((0,), (0,)), ((), ())), preferred_element_type=jnp.float32
    )


def times_transpose(left, right):
    return lax.dot_general(
        left, right, (((1,), (1,)), ((), ())), preferred_element_type=jnp.float32
    )


def gelu_slope(values):
    return 0.5 * (1.0 + jax.scipy.special.erf(values / math.sqrt(2.0))) + values * jnp.exp(
        -0.5 * values * values
    ) / math.sqrt(2.0 * math.pi)


def wave_features(wavelengths, wave_index):
    table_size = wavelengths.shape[0]
    picked = (wave_index[..., None] == jnp.arange(table_size, dtype=jnp.int32)).astype(jnp.float32)
    wave_values = jnp.sum(picked * wavelengths, axis=-1)
    half_width = WG // 2
    frequency = 1.0 / 10000.0 ** (jnp.arange(half_width, dtype=jnp.float32) / half_width)
    angles = 1000.0 * wave_values[..., None] * frequency
    return jnp.concatenate([jnp.sin(angles), jnp.cos(angles)], axis=-1)


def generator(gen_params, features, band_valid):
    gen_qkv, gen_out, gen_ff1, gen_ff2, gen_gains, gen_shifts, latent_tokens, bias_token = (
        gen_params
    )
    sensor_count = features.shape[0]
    sequence = jnp.concatenate(
        [
            jnp.broadcast_to(latent_tokens, (sensor_count, NLAT, WG)),
            features,
            jnp.broadcast_to(bias_token, (sensor_count, 1, WG)),
        ],
        axis=1,
    )
    key_valid = jnp.concatenate(
        [
            jnp.ones((sensor_count, NLAT), jnp.bool_),
            band_valid,
            jnp.ones((sensor_count, 1), jnp.bool_),
        ],
        axis=1,
    )
    seq_length = sequence.shape[1]
    projected = jnp.einsum("slw,wk->slk", sequence, gen_qkv, precision=exact_precision)
    projected = projected.reshape(sensor_count, seq_length, 3, GHEADS, GHD)
    scores = jnp.einsum(
        "sqhd,skhd->shqk", projected[:, :, 0], projected[:, :, 1], precision=exact_precision
    ) / math.sqrt(GHD)
    scores = jnp.where(key_valid[:, None, None, :], scores, masked_score)
    attention = jax.nn.softmax(scores, axis=-1)
    mixed_heads = jnp.einsum(
        "shqk,skhd->sqhd", attention, projected[:, :, 2], precision=exact_precision
    )
    mixed_heads = mixed_heads.reshape(sensor_count, seq_length, WG)
    first_norm = layer_norm(
        sequence + jnp.einsum("slw,wk->slk", mixed_heads, gen_out, precision=exact_precision),
        gen_gains[0],
        gen_shifts[0],
    )
    inner_act = jax.nn.gelu(
        jnp.einsum("slw,wf->slf", first_norm, gen_ff1, precision=exact_precision), approximate=False
    )
    second = layer_norm(
        first_norm + jnp.einsum("slf,fw->slw", inner_act, gen_ff2, precision=exact_precision),
        gen_gains[1],
        gen_shifts[1],
    )
    band_rows = second[:, NLAT : NLAT + BMAX] + features
    return (band_rows, second[:, -1])


def shards(
    pixels,
    wavelengths,
    wave_index,
    band_counts,
    sensors,
    chip_lengths,
    meta_rows,
    w_qkv,
    w_out,
    w_up,
    b_up,
    w_down,
    norm_gains,
    shifts,
    gen_qkv,
    gen_out,
    gen_ff1,
    gen_ff2,
    gen_gains,
    gen_shifts,
    latent_tokens,
    bias_token,
    fc_kernel,
    fc_bias,
    d_out,
):
    band_size = lax.axis_size("band")
    band_index = lax.axis_index("band")
    tok_size = lax.axis_size("tok")
    tok_index = lax.axis_index("tok")
    shard_index = band_index * tok_size + tok_index
    device_total = band_size * tok_size
    slots_own = BMAX // band_size
    frame_local = meta_rows.shape[1]
    groups = pixels.shape[0]
    pixel_width = pixels.shape[3]
    score_scale = 1.0 / math.sqrt(HD)
    features = wave_features(wavelengths, wave_index)
    band_valid = jnp.arange(BMAX, dtype=jnp.int32)[None, :] < band_counts[:, None]
    own_valid = lax.dynamic_slice_in_dim(band_valid, band_index * slots_own, slots_own, 1)
    gen_params = (
        gen_qkv,
        gen_out,
        gen_ff1,
        gen_ff2,
        gen_gains,
        gen_shifts,
        latent_tokens,
        bias_token,
    )

    def own_generator(params_all):
        band_rows, last_rows = generator(params_all, features, band_valid)
        return (
            lax.dynamic_slice_in_dim(band_rows, band_index * slots_own, slots_own, 1),
            last_rows,
        )

    (own_rows, last_rows), gen_pullback = jax.vjp(own_generator, gen_params)
    own_flat = own_rows.reshape(SENSORS * slots_own, WG)
    valid_column = own_valid.reshape(SENSORS * slots_own, 1).astype(jnp.float32)
    kernel_part = (jnp.dot(own_flat, fc_kernel, precision=exact_precision) * valid_column).astype(
        jnp.bfloat16
    )
    kernel_own = lax.all_gather(kernel_part, "tok", axis=1, tiled=True).reshape(
        SENSORS, slots_own * PIX, D
    )
    bias_vec = jnp.dot(last_rows, fc_bias, precision=exact_precision)
    chip_ends = jnp.cumsum(chip_lengths.reshape(-1, CAP), axis=-1)
    block_starts = jnp.arange(CAP, dtype=jnp.int32) * CHIP
    block_segment = jnp.sum(
        (chip_ends[:, None, :] <= block_starts[None, :, None]).astype(jnp.int32), axis=-1
    )
    block_sensor = jnp.take_along_axis(sensors.reshape(-1, CAP), block_segment, axis=1)
    sensor_flat = block_sensor.reshape(-1)
    own_ends = lax.dynamic_slice_in_dim(
        chip_ends.reshape(groups, frame_local, CAP), band_index, 1, 0
    ).reshape(frame_local, CAP)
    own_sensor = lax.dynamic_slice_in_dim(
        block_sensor.reshape(groups, frame_local, CAP), band_index, 1, 0
    ).reshape(frame_local * CAP)
    positions = jnp.arange(FRAME, dtype=jnp.int32)
    patch_segment = jnp.sum(
        (own_ends[:, None, :] <= positions[None, :, None]).astype(jnp.int32), axis=-1
    )
    extra_segment = jnp.broadcast_to(jnp.arange(CAP, dtype=jnp.int32), (frame_local, CAP))
    row_segment = jnp.concatenate([patch_segment, extra_segment, extra_segment], axis=1)
    pixel_rows = pixels.reshape(-1, pixel_width)
    block_total = frame_local * FRAME * lax.axis_size("band") // CHIP
    pixel_portion = pixel_rows.reshape(block_total, CHIP, pixel_width)
    selected_entries = jnp.take(kernel_own, sensor_flat, axis=0)
    embed_sum = lax.psum_scatter(
        jnp.einsum(
            "qis,qse->qie", pixel_portion, selected_entries, preferred_element_type=jnp.float32
        )
        .reshape(frame_local * FRAME * lax.axis_size("band"), D)
        .astype(jnp.bfloat16),
        "band",
        scatter_dimension=0,
        tiled=True,
    ).astype(jnp.float32)
    bias_rows = jnp.take(bias_vec, own_sensor, axis=0)
    embedded = (embed_sum.reshape(frame_local * CAP, CHIP, D) + bias_rows[:, None, :]).reshape(
        frame_local, FRAME, D
    )
    gathered_qkv, gathered_out, gains_all, shifts_all = (
        lax.all_gather(w_qkv, ("band", "tok"), axis=0, tiled=True),
        lax.all_gather(w_out, ("band", "tok"), axis=0, tiled=True),
        lax.all_gather(norm_gains, ("band", "tok"), axis=1, tiled=True),
        lax.all_gather(shifts, ("band", "tok"), axis=1, tiled=True),
    )
    gains_full = gains_all.astype(jnp.float32)
    shifts_full = shifts_all.astype(jnp.float32)
    class_rows = jnp.broadcast_to(shifts_full[3], (frame_local, CAP, D))
    stream = jnp.concatenate(
        [embedded, class_rows, meta_rows[0].astype(jnp.float32)], axis=1
    ).reshape(frame_local * ROWS, D)
    normed_one, hat_one, scale_one = norm_forward(stream, gains_full[0], shifts_full[0])
    normed_one = normed_one.astype(jnp.bfloat16)
    projected = jnp.dot(normed_one, gathered_qkv, preferred_element_type=jnp.float32).astype(
        jnp.bfloat16
    )
    head_major = (
        projected.reshape(frame_local, ROWS, 3, HEADS, HD)
        .transpose(2, 0, 3, 1, 4)
        .reshape(3, frame_local * HEADS, ROWS, HD)
    )
    segment_heads = jnp.repeat(row_segment, HEADS, axis=0)

    def head_forward(inputs):
        query_rows, key_rows, value_rows, segment_row = inputs
        scores = times_transpose(query_rows, key_rows) * score_scale
        same_chip = segment_row[:, None] == segment_row[None, :]
        scores = jnp.where(same_chip, scores, masked_score)
        row_max = jnp.max(scores, axis=-1, keepdims=True)
        exponent = jnp.exp(scores - row_max)
        row_total = jnp.sum(exponent, axis=-1, keepdims=True)
        probabilities = (exponent / row_total).astype(jnp.bfloat16)
        mixed_rows = jnp.dot(probabilities, value_rows, preferred_element_type=jnp.float32)
        return (mixed_rows.astype(jnp.bfloat16), (row_max + jnp.log(row_total))[:, 0])

    attended_heads, log_totals = lax.map(
        head_forward, (head_major[0], head_major[1], head_major[2], segment_heads)
    )
    attended = (
        attended_heads.reshape(frame_local, HEADS, ROWS, HD)
        .transpose(0, 2, 1, 3)
        .reshape(frame_local * ROWS, D)
    )
    middle = stream + jnp.dot(attended, gathered_out, preferred_element_type=jnp.float32)
    up_all, bias_up_all, down_all = (
        lax.all_gather(w_up, ("band", "tok"), axis=0, tiled=True),
        lax.all_gather(b_up, ("band", "tok"), axis=0, tiled=True),
        lax.all_gather(w_down, ("band", "tok"), axis=0, tiled=True),
    )
    normed_two, hat_two, scale_two = norm_forward(middle, gains_full[1], shifts_full[1])
    normed_two = normed_two.astype(jnp.bfloat16)
    hidden_pre = jnp.dot(
        normed_two, up_all, preferred_element_type=jnp.float32
    ) + bias_up_all.astype(jnp.float32)
    activated = jax.nn.gelu(hidden_pre, approximate=False).astype(jnp.bfloat16)
    result = (
        middle + jnp.dot(activated, down_all, preferred_element_type=jnp.float32) + shifts_full[2]
    )
    grad_top = d_out[0].reshape(frame_local * ROWS, D)
    grad_stream = grad_top.astype(jnp.float32)
    grad_down_shard = lax.psum_scatter(
        contract_rows(activated, grad_top), ("band", "tok"), scatter_dimension=0, tiled=True
    )
    grad_down_shift = jnp.sum(grad_stream, axis=0)
    grad_act = times_transpose(grad_top, down_all).astype(jnp.bfloat16)
    grad_pre = (grad_act.astype(jnp.float32) * gelu_slope(hidden_pre)).astype(jnp.bfloat16)
    grad_bias_up = jnp.sum(grad_pre, axis=0, dtype=jnp.float32)
    grad_normed_two = times_transpose(grad_pre, up_all)
    grad_in_two, grad_gain_two, grad_shift_two = norm_backward(
        grad_normed_two, hat_two, scale_two, gains_full[1]
    )
    grad_middle = grad_stream + grad_in_two
    grad_middle_low = grad_middle.astype(jnp.bfloat16)
    grad_attended = times_transpose(grad_middle_low, gathered_out).astype(jnp.bfloat16)
    grad_heads = (
        grad_attended.reshape(frame_local, ROWS, HEADS, HD)
        .transpose(0, 2, 1, 3)
        .reshape(frame_local * HEADS, ROWS, HD)
    )

    def head_backward(inputs):
        query_rows, key_rows, value_rows, segment_row, log_total, grad_mixed = inputs
        scores = times_transpose(query_rows, key_rows) * score_scale
        same_chip = segment_row[:, None] == segment_row[None, :]
        probabilities = jnp.where(same_chip, jnp.exp(scores - log_total[:, None]), 0.0)
        probs_low = probabilities.astype(jnp.bfloat16)
        grad_value = contract_rows(probs_low, grad_mixed)
        grad_probs = times_transpose(grad_mixed, value_rows)
        row_inner = jnp.sum(probabilities * grad_probs, axis=-1, keepdims=True)
        grad_scores = (probabilities * (grad_probs - row_inner)).astype(jnp.bfloat16)
        grad_query = (
            jnp.dot(grad_scores, key_rows, preferred_element_type=jnp.float32) * score_scale
        )
        grad_key = contract_rows(grad_scores, query_rows) * score_scale
        return (
            grad_query.astype(jnp.bfloat16),
            grad_key.astype(jnp.bfloat16),
            grad_value.astype(jnp.bfloat16),
        )

    grad_query_all, grad_key_all, grad_value_all = lax.map(
        head_backward,
        (head_major[0], head_major[1], head_major[2], segment_heads, log_totals, grad_heads),
    )
    grad_qkv = jnp.stack([grad_query_all, grad_key_all, grad_value_all]).reshape(
        3, frame_local, HEADS, ROWS, HD
    )
    grad_qkv = grad_qkv.transpose(1, 3, 0, 2, 4).reshape(frame_local * ROWS, 3 * D)
    grad_normed_one = times_transpose(grad_qkv, gathered_qkv)
    weight_shard = lax.psum_scatter(
        jnp.concatenate(
            [
                contract_rows(normed_one, grad_qkv),
                contract_rows(attended, grad_middle_low),
                contract_rows(normed_two, grad_pre),
            ],
            axis=1,
        ),
        ("band", "tok"),
        scatter_dimension=0,
        tiled=True,
    )
    grad_in_one, grad_gain_one, grad_shift_one = norm_backward(
        grad_normed_one, hat_one, scale_one, gains_full[0]
    )
    grad_first = (grad_middle + grad_in_one).reshape(frame_local, ROWS, D)
    grad_class = jnp.sum(grad_first[:, FRAME : FRAME + CAP], axis=(0, 1))
    grad_meta = grad_first[:, FRAME + CAP :][None]
    grad_gains = jnp.stack([grad_gain_one, grad_gain_two])
    grad_shifts = jnp.stack([grad_shift_one, grad_shift_two, grad_down_shift, grad_class])
    grad_embed = grad_first[:, :FRAME].astype(jnp.bfloat16)
    own_blocks = grad_embed.reshape(frame_local * CAP, CHIP, D)
    own_onehot = (own_sensor[:, None] == jnp.arange(SENSORS, dtype=jnp.int32)[None, :]).astype(
        jnp.float32
    )
    block_sums = jnp.sum(own_blocks, axis=1, dtype=jnp.float32)
    grad_bias_vec = jnp.einsum("bs,bd->sd", own_onehot, block_sums, precision=exact_precision)
    gathered_grad = lax.all_gather(grad_embed[None], "band", axis=0, tiled=True)
    gradient_block_rows = gathered_grad.reshape(-1, CHIP, D)
    pixel_block_rows = pixels.reshape(-1, CHIP, pixel_width)
    block_kernel_matrix = jnp.take(kernel_own, sensor_flat, axis=0)
    grad_pixels = jnp.einsum(
        "ngf,nuf->ngu", gradient_block_rows, block_kernel_matrix, preferred_element_type=jnp.float32
    ).reshape(pixels.shape)
    block_gradient_list = jnp.einsum(
        "aye,ayw->aew", pixel_block_rows, gradient_block_rows, preferred_element_type=jnp.float32
    )
    every_onehot_table = (
        sensor_flat[:, None] == jnp.arange(SENSORS, dtype=jnp.int32)[None, :]
    ).astype(jnp.float32)
    kernel_gradient = jnp.einsum(
        "oq,oxy->qxy", every_onehot_table, block_gradient_list, precision=exact_precision
    )
    kernel_gradient = kernel_gradient.reshape(SENSORS * slots_own, PIX * D) * valid_column
    kernel_cols = lax.psum_scatter(kernel_gradient, "tok", scatter_dimension=1, tiled=True)
    fc_part = jnp.einsum("nw,nc->wc", own_flat, kernel_cols, precision=exact_precision)
    grad_fc_kernel = lax.psum(fc_part.astype(jnp.bfloat16), "band").astype(jnp.float32)
    grad_rows = jnp.einsum("nc,wc->nw", kernel_cols, fc_kernel, precision=exact_precision).reshape(
        SENSORS, slots_own, WG
    )
    grad_fc_bias = jnp.einsum("sw,sd->wd", last_rows, grad_bias_vec, precision=exact_precision)
    grad_last = jnp.einsum("sd,wd->sw", grad_bias_vec, fc_bias, precision=exact_precision)
    (gen_grads,) = gen_pullback((grad_rows, grad_last))
    summed = lax.psum(
        (
            gen_grads[0],
            gen_grads[1],
            gen_grads[2],
            gen_grads[3],
            gen_grads[4],
            gen_grads[5],
            gen_grads[6],
            gen_grads[7],
            grad_fc_bias,
            grad_bias_up,
            grad_gains,
            grad_shifts,
        ),
        ("band", "tok"),
    )
    ff_share = FF // device_total
    d_share = D // device_total
    bias_up_shard = lax.dynamic_slice_in_dim(summed[9], shard_index * ff_share, ff_share, 0)
    gains_shard = lax.dynamic_slice_in_dim(summed[10], shard_index * d_share, d_share, 1)
    shifts_shard = lax.dynamic_slice_in_dim(summed[11], shard_index * d_share, d_share, 1)
    return (
        result.reshape(1, frame_local, ROWS, D),
        grad_pixels,
        grad_meta,
        weight_shard[:, : 3 * D],
        weight_shard[:, 3 * D : 4 * D],
        weight_shard[:, 4 * D :],
        bias_up_shard,
        grad_down_shard,
        gains_shard,
        shifts_shard,
        summed[0],
        summed[1],
        summed[2],
        summed[3],
        summed[4],
        summed[5],
        summed[6],
        summed[7],
        grad_fc_kernel,
        summed[8],
    )


def solution(mesh):
    placed = (
        P(None, "tok", None, "band"),
        P(),
        P(),
        P(),
        P(None, "tok", None),
        P(None, "tok", None),
        P("band", "tok", None, None),
        P(("band", "tok"), None),
        P(("band", "tok"), None),
        P(("band", "tok"), None),
        P(("band", "tok")),
        P(("band", "tok"), None),
        P(None, ("band", "tok")),
        P(None, ("band", "tok")),
        P(),
        P(),
        P(),
        P(),
        P(),
        P(),
        P(),
        P(),
        P(None, "tok"),
        P(),
        P("band", "tok", None, None),
    )
    return jax.shard_map(
        shards,
        mesh=mesh,
        in_specs=placed,
        out_specs=(
            P("band", "tok", None, None),
            P(None, "tok", None, "band"),
            P("band", "tok", None, None),
            P(("band", "tok"), None),
            P(("band", "tok"), None),
            P(("band", "tok"), None),
            P(("band", "tok")),
            P(("band", "tok"), None),
            P(None, ("band", "tok")),
            P(None, ("band", "tok")),
            P(),
            P(),
            P(),
            P(),
            P(),
            P(),
            P(),
            P(),
            P(None, "tok"),
            P(),
        ),
        check_vma=False,
    )
```

profile of v0, /device:TPU:0, one launch (start us, length us, event | category | flops | bytes accessed | tf_op | source)
XLA Modules:
  0.0 1217.7 jit_solution(14034500981859481493)
XLA Ops:
  12.7 3.5 fusion.120
  16.2 4.7 fusion.81
  22.2 3.4 fusion.91
  28.3 10.9 fusion.87
  39.3 17.8 %fusion.72 = f32[7,141,2048]{2,1,0:T(8,128)S(1)} fusion(f32[7,141,2048]{2,1,0:T(8,128)S(1)} %get-tuple-element.365, u8[141,2048]{1,0:T(8,128)(4,1)S(1)} %get-tuple-element.267, u8[141,2048]{1,0:T(8,128)(4,1)S(1)} %get-tuple-element.268, u8[141,2048]{1,0:T(8,128)(4,1)S(1)} %get-tuple-element.266), kind=kLoop, calls=%fused_computation.97 | loop fusion | flops 139474944 | bytes 17037312 | tf_op jit(solution)/shard_map/jvp()/erfc | solution.py:122
  57.1 6.8 fusion.180
  70.3 3.8 copy.165
  74.1 3.8 reshape_reshape.3
  79.1 24.2 %all-gather.10.cloned.1.call-done = bf16[21,49152]{1,0:T(8,128)(2,1)} async-done(((bf16[21,6144]{1,0:T(8,128)(2,1)}), bf16[21,49152]{1,0:T(8,128)(2,1)}) %all-gather.10.cloned.1.call-update) | async-done | bytes 2064400 | tf_op jit(solution)/shard_map/all_gather | solution.py:199
  103.4 4.7 reshape.565
  108.1 4.6 gather_fusion.2
  112.6 7.7 convolution_convert_fusion.3
  129.9 42.6 %all-gather.1 = bf16[32,24,4]{1,2,0:T(4,128)(2,1)} all-gather(bf16[1,24,4]{1,2,0:T(4,128)(2,1)} %bitcast.370), channel_id=1, replica_groups=mesh['band'=4,'tok'=8] {'band','tok'}, dimensions={0}, use_global_device_ids=true | all-gather | bytes 6336 | tf_op jit(solution)/shard_map/all_gather | solution.py:244
  179.7 37.9 %all-gather.2 = bf16[32,24,2]{1,2,0:T(2,128)(2,1)} all-gather(bf16[1,24,2]{1,2,0:T(2,128)(2,1)} %bitcast.371), channel_id=1, replica_groups=mesh['band'=4,'tok'=8] {'band','tok'}, dimensions={0}, use_global_device_ids=true | all-gather | bytes 3168 | tf_op jit(solution)/shard_map/all_gather | solution.py:243
  225.3 40.6 %all-reduce.9 = bf16[3072]{0:T(1024)(128)(2,1)} all-reduce(bf16[3072]{0:T(1024)(128)(2,1)} %dynamic-update-slice), channel_id=1, replica_groups=mesh['band'=4,'tok'=8] {'band','tok'}, use_global_device_ids=true, to_apply=%add.9 | all-reduce | flops 3072 | bytes 12288
  273.6 8.5 concatenate.29
  286.8 9.4 convolution_convert_fusion.1
  296.2 8.4 copy.171
  304.6 5.7 slice_bitcast_fusion
  310.4 4.5 copy.172
  314.8 4.5 copy.173
  319.3 4.5 copy.174
  325.2 80.6 %while.26 = (s32[]{:T(128)}, bf16[12,1032,64]{1,2,0:T(8,128)(2,1)}, f32[12,1032]{1,0:T(8,128)}, s32[12,1032]{1,0:T(8,128)S(1)}, bf16[12,1032,64]{2,1,0:T(8,128)(...) while((s32[]{:T(128)}, bf16[12,1032,64]{1,2,0:T(8,128)(2,1)}, ...), condition=%wide.region_16.18_spmd, body=%wide.region_13.17_spmd.sunk | while | flops 282296384 | bytes 13796653 | solution.py:276
  405.9 5.9 fusion.181
  414.3 37.0 %fusion.56 = (bf16[1032,3072]{1,0:T(8,128)(2,1)}, f32[1032,3072]{1,0:T(8,128)}) fusion(f32[3072]{0:T(1024)S(1)} %copy-done.84, bf16[768,3072]{1,0:T(8,128)(2,1)} %all-gather.16.cloned.1.call-done, f32[1032,768]{1,0:T(8,128)} %get-tuple-element.369, f32[768]{0:T(1024)S(1)} %get-tuple-element.285, f32[768]{0:T(1024)S(1)} %get-tuple-element.288, ...), kind=kOutput, calls=%fused_computation.69 | convolution fusion | flops 5082789888 | bytes 26937408 | tf_op jit(solution)/shard_map/dot_general | solution.py:292
  451.3 12.7 %convert_reduce_fusion = (f32[3072]{0:T(1024)}, bf16[1032,3072]{1,0:T(8,128)(2,1)S(1)}) fusion(f32[1032,3072]{1,0:T(8,128)} %get-tuple-element.371, bf16[3072,768]{1,0:T(8,128)(2,1)} %all-gather.18.cloned.1.call-done, bf16[1,1,1032,768]{3,2,1,0:T(8,128)(2,1)} %param.55), kind=kOutput, calls=%fused_computation.76 | convolution fusion | flops 4913968128 | bytes 25337856 | tf_op jit(solution)/shard_map/dot_general | solution.py:63
  464.0 10.7 multiply_reduce_fusion.2
  474.7 3.5 convert_reduce_fusion.1
  482.7 3.8 copy.175
  490.8 167.8 %while.27 = (s32[]{:T(128)}, bf16[12,1032,64]{1,2,0:T(8,128)(2,1)}, bf16[12,1032,64]{1,2,0:T(8,128)(2,1)}, bf16[12,1032,64]{1,2,0:T(8,128)(2,1)}, s32[12,1032]{1...) while((s32[]{:T(128)}, bf16[12,1032,64]{1,2,0:T(8,128)(2,1)}, ...), condition=%wide.region_23.25_spmd, body=%wide.region_21.24_spmd.sunk | while | flops 692594816 | bytes 34558908 | solution.py:341
  658.6 4.4 pad_maximum_fusion.1
  663.2 6.1 multiply_reduce_fusion.3
  673.9 68.8 %all-gather.20.cloned.1.call-done = bf16[4,1024,768]{2,1,0:T(8,128)(2,1)} async-done(((bf16[1,1024,768]{2,1,0:T(8,128)(2,1)}), bf16[4,1024,768]{2,1,0:T(8,128)(2,1)}) %all-gather.20.cloned.1.call-update) | async-done | bytes 6291472 | tf_op jit(solution)/shard_map/all_gather | solution.py:378
  742.7 5.0 convolution_bitcast_fusion
  747.7 8.9 fusion.70
  756.7 3.7 copy.184
  760.4 5.1 reshape.583
  765.5 4.9 broadcast_multiply_fusion
  771.1 8.7 concatenate.32
  779.9 11.8 fusion.92
  791.6 12.4 %fusion.175 = f32[768,3072]{1,0:T(8,128)} fusion(bf16[1032,3072]{1,0:T(8,128)(2,1)} %copy-done.16, f32[1032,768]{1,0:T(8,128)} %get-tuple-element.369, f32[768]{0:T(1024)S(1)} %get-tuple-element.285, f32[768]{0:T(1024)S(1)} %get-tuple-element.288, f32[1032]{0:T(1024)S(1)} %add_rsqrt_fusion, f32[1032]{0:T(1024)S(1)} %broadcast_multiply_fusion.5), kind=kOutput, calls=%fused_computation.347 | convolution fusion | flops 4873549824 | bytes 18962496 | tf_op jit(solution)/shard_map/dot_general | solution.py:57
  804.1 21.5 %reduce-scatter.11.cloned.1.call-done = f32[21,6144]{1,0:T(8,128)} async-done(((f32[21,49152]{1,0:T(8,128)}), f32[21,6144]{1,0:T(8,128)}) %reduce-scatter.11.cloned.1.call-update) | async-done | bytes 516112 | tf_op jit(solution)/shard_map/reduce_scatter | solution.py:395
  825.6 4.9 convolution_convert_fusion.2
  830.7 4.3 fusion.115
  836.4 9.6 pad_maximum_fusion
  846.0 11.2 fusion.93
  866.8 11.1 fusion.80
  884.3 15.3 %multiply_add_fusion = f32[7,141,2048]{2,1,0:T(8,128)S(1)} fusion(f32[7,141,2048]{2,1,0:T(8,128)} %copy-done.3, f32[7,141,2048]{2,1,0:T(8,128)} %copy-done.2, f32[2048,128]{1,0:T(8,128)} %param.48, f32[7,141]{1,0:T(8,128)S(1)} %negate_multiply_fusion.3, f32[7,12,128]{2,1,0:T(8,128)S(1)} %dynamic_update_slice.20, f32[7,1,128]{2,1,0:T(1,128)S(1)} %broadcast_in_dim.176, ...), kind=kOutput, calls=%fused_computation.105 | convolution fusion | flops 3132122112 | bytes 25873328 | tf_op jit(solution)/shard_map/transpose(jvp(slf,fw->slw))/dot_general | solution.py:126
  899.7 6.9 multiply_reduce_fusion.10
  908.6 5.6 multiply_reduce_fusion.1
  919.0 4.3 convolution_bitcast_fusion.3
  923.3 4.9 fusion.106
  929.1 5.0 convolution_add_fusion.4
  936.6 4.0 convolution_bitcast_fusion.4
  940.6 5.7 convolution_bitcast_fusion.1
  946.3 15.3 %fusion.85 = f32[2048,128]{1,0:T(8,128)} fusion(f32[7,141,2048]{2,1,0:T(8,128)S(1)} %bitcast.336, f32[7,141,2048]{2,1,0:T(8,128)S(1)} %bitcast.334, f32[7,141]{1,0:T(8,128)S(1)} %negate_multiply_fusion.3, f32[7,12,128]{2,1,0:T(8,128)S(1)} %dynamic_update_slice.20, f32[7,1,128]{2,1,0:T(1,128)S(1)} %broadcast_in_dim.176, f32[7,141,128]{2,1,0:T(8,128)S(1)} %copy-done.9, ...), kind=kOutput, calls=%fused_computation.159 | convolution fusion | flops 3109886976 | bytes 17787824 | tf_op jit(solution)/shard_map/transpose(jvp(slf,fw->slw))/dot_general | solution.py:126
  961.7 6.4 fusion.89
  968.2 3.5 copy.180
  971.6 5.2 reshape.582
  976.8 5.4 copy.193
  983.0 41.7 %all-reduce.10 = (f32[3072]{0:T(1024)S(1)}, f32[2,768]{1,0:T(2,128)S(1)}, f32[4,768]{1,0:T(4,128)S(1)}, f32[2,128]{1,0:T(2,128)}, f32[2,128]{1,0:T(2,128)}, /*index=5*/f32[128]{0:T(128)}) all-reduce(f32[3072]{0:T(1024)S(1)} %copy-done.83, f32[2,768]{1,0:T(2,128)S(1)} %pad_maximum_fusion.6, ...), channel_id=1, replica_groups=mesh['band'=4,'tok'=8] {'band','tok'}, use_global_device_ids=true, to_apply=%region_28.30 | all-reduce | flops 8320 | bytes 66560 | tf_op jit(solution)/shard_map/psum | solution.py:404
  1026.7 3.4 convert_element_type.181
  1030.0 26.0 %reduce-scatter.7.cloned.1.call-done = f32[24,6144]{1,0:T(8,128)} async-done(((f32[768,6144]{1,0:T(8,128)}), f32[24,6144]{1,0:T(8,128)}) %reduce-scatter.7.cloned.1.call-update) | async-done | bytes 589840 | tf_op jit(solution)/shard_map/reduce_scatter | solution.py:350
  1060.9 140.0 %reduce-scatter.9.cloned.1.call-done = f32[96,768]{1,0:T(8,128)} async-done(((f32[3072,768]{1,0:T(8,128)}), f32[96,768]{1,0:T(8,128)}) %reduce-scatter.9.cloned.1.call-update) | async-done | bytes 294928 | tf_op jit(solution)/shard_map/reduce_scatter | solution.py:301
  (564 shorter events, 362.7 us)
Async XLA Ops:
  8.0 58.5 %copy-start = (f32[128,6144]{1,0:T(8,128)S(1)}, f32[128,6144]{1,0:T(8,128)}, u32[]{:S(2)}) copy-start(f32[128,6144]{1,0:T(8,128)} %param.53) | copy-start | bytes 9437188
  8.0 95.3 %all-gather.10.cloned.1.call-start = ((), (), s32[]{:S(2)}) async-start(), calls=%async_computation.4 | async-start | bytes 2654208 | tf_op jit(solution)/shard_map/all_gather | solution.py:199
  11.1 55.3 %copy-start.28 = (f32[7,12,64]{2,1,0:T(8,128)}, f32[7,12,64]{2,1,0:T(8,128)S(1)}, u32[]{:S(2)}) copy-start(f32[7,12,64]{2,1,0:T(8,128)S(1)} %get-tuple-element.355) | copy-start | bytes 64516
  11.1 55.3 %copy-start.30 = (f32[7,12,64]{2,1,0:T(8,128)}, f32[7,12,64]{2,1,0:T(8,128)S(1)}, u32[]{:S(2)}) copy-start(f32[7,12,64]{2,1,0:T(8,128)S(1)} %get-tuple-element.356) | copy-start | bytes 64516
  11.1 11.0 copy-start.65
  11.8 13.8 %copy-start.63 = (f32[7,1,128]{2,1,0:T(1,128)}, f32[7,1,128]{2,1,0:T(1,128)S(1)}, u32[]{:S(2)}) copy-start(f32[7,1,128]{2,1,0:T(1,128)S(1)} %broadcast_in_dim.165) | copy-start | bytes 10756
  12.7 13.0 %copy-start.17 = (f32[7,128,128]{2,1,0:T(8,128)}, f32[7,128,128]{2,1,0:T(8,128)S(1)}, u32[]{:S(2)}) copy-start(f32[7,128,128]{2,1,0:T(8,128)S(1)} %broadcast_in_dim.164) | copy-start | bytes 1376260
  25.6 13.7 %copy-start.21 = (f32[7,4,32,141]{3,2,1,0:T(8,128)}, f32[7,4,32,141]{3,2,1,0:T(8,128)S(1)}, u32[]{:S(2)}) copy-start(f32[7,4,32,141]{3,2,1,0:T(8,128)S(1)} %fusion.91) | copy-start | bytes 1516036
  27.7 29.4 %copy-start.12 = (f32[7,141,128]{2,1,0:T(8,128)}, f32[7,141,128]{2,1,0:T(8,128)S(1)}, u32[]{:S(2)}) copy-start(f32[7,141,128]{2,1,0:T(8,128)S(1)} %get-tuple-element.364) | copy-start | bytes 1516036
  27.7 29.4 %copy-start.42 = (f32[7,141]{1,0:T(8,128)}, f32[7,141]{1,0:T(8,128)S(1)}, u32[]{:S(2)}) copy-start(f32[7,141]{1,0:T(8,128)S(1)} %broadcast_multiply_fusion.8) | copy-start | bytes 11848
  28.2 11.1 copy-start.56
  28.2 28.8 %copy-start.50 = (f32[7,141]{1,0:T(8,128)}, f32[7,141]{1,0:T(8,128)S(1)}, u32[]{:S(2)}) copy-start(f32[7,141]{1,0:T(8,128)S(1)} %fusion.145) | copy-start | bytes 11848
  28.3 28.8 %copy-start.81 = (f32[128]{0:T(128)}, f32[128]{0:T(128)S(1)}, u32[]{:S(2)}) copy-start(f32[128]{0:T(128)S(1)} %get-tuple-element.379) | copy-start | bytes 1540
  28.3 28.8 %copy-start.88 = (f32[128]{0:T(128)}, f32[128]{0:T(128)S(1)}, u32[]{:S(2)}) copy-start(f32[128]{0:T(128)S(1)} %get-tuple-element.360) | copy-start | bytes 1540
  28.3 36.8 %copy-start.76 = (f32[128]{0:T(128)}, f32[128]{0:T(128)S(1)}, u32[]{:S(2)}) copy-start(f32[128]{0:T(128)S(1)} %get-tuple-element.380) | copy-start | bytes 1540
  39.3 17.8 %copy-start.2 = (f32[7,141,2048]{2,1,0:T(8,128)}, f32[7,141,2048]{2,1,0:T(8,128)S(1)}, u32[]{:S(2)}) copy-start(f32[7,141,2048]{2,1,0:T(8,128)S(1)} %get-tuple-element.365) | copy-start | bytes 24256516
  39.3 17.8 %copy-start.32 = (f32[2048,128]{1,0:T(8,128)S(1)}, f32[2048,128]{1,0:T(8,128)}, u32[]{:S(2)}) copy-start(f32[2048,128]{1,0:T(8,128)} %param.48) | copy-start | bytes 3145732
  66.5 11.3 copy-start.1
  68.9 201.4 %reduce-scatter.5.cloned.1.call-start = ((), (), s32[]{:S(2)}) async-start(), calls=%async_computation.5 | async-start | bytes 7864320 | tf_op jit(solution)/shard_map/reduce_scatter | solution.py:226
  78.5 34.1 %copy-start.98 = (pred[16]{0:T(512)(128)(4,1)}, pred[16]{0:T(512)(128)(4,1)S(1)}, u32[]{:S(2)}) copy-start(pred[16]{0:T(512)(128)(4,1)S(1)} %get-tuple-element.340) | copy-start | bytes 52
  120.3 146.9 %copy-start.26 = (f32[128,768]{1,0:T(8,128)S(1)}, f32[128,768]{1,0:T(8,128)}, u32[]{:S(2)}) copy-start(f32[128,768]{1,0:T(8,128)} %param.54) | copy-start | bytes 1179652
  120.3 166.4 %all-gather.12.cloned.1.call-start = ((), (), s32[]{:S(2)}) async-start(), calls=%async_computation.6 | async-start | bytes 3649536 | tf_op jit(solution)/shard_map/all_gather | solution.py:241
  120.9 284.9 %all-gather.14.cloned.1.call-start = ((), (), s32[]{:S(2)}) async-start(), calls=%async_computation.7 | async-start | bytes 1216512 | tf_op jit(solution)/shard_map/all_gather | solution.py:242
  121.5 292.7 %all-gather.16.cloned.1.call-start = ((), (), s32[]{:S(2)}) async-start(), calls=%async_computation.8 | async-start | bytes 4866048 | tf_op jit(solution)/shard_map/all_gather | solution.py:286
  122.1 329.2 %all-gather.18.cloned.1.call-start = ((), (), s32[]{:S(2)}) async-start(), calls=%async_computation.9 | async-start | bytes 4866048 | tf_op jit(solution)/shard_map/all_gather | solution.py:288
  122.8 619.9 %all-gather.20.cloned.1.call-start = ((), (), s32[]{:S(2)}) async-start(), calls=%async_computation.14 | async-start | bytes 7864320 | tf_op jit(solution)/shard_map/all_gather | solution.py:378
  123.6 158.5 %copy-start.69 = (f32[7,1,128]{2,1,0:T(1,128)}, f32[7,1,128]{2,1,0:T(1,128)S(1)}, u32[]{:S(2)}) copy-start(f32[7,1,128]{2,1,0:T(1,128)S(1)} %slice.115) | copy-start | bytes 10756
  178.4 103.7 %copy-start.71 = (f32[768]{0:T(1024)}, f32[768]{0:T(1024)S(1)}, u32[]{:S(2)}) copy-start(f32[768]{0:T(1024)S(1)} %get-tuple-element.287) | copy-start | bytes 9220
  284.3 11.9 copy-start.60
  286.7 9.5 copy-start.74
  314.8 8.9 copy-start.73
  405.9 8.4 copy-start.84
  451.3 12.7 %copy-start.100 = (bf16[768,3072]{1,0:T(8,128)(2,1)S(1)}, bf16[768,3072]{1,0:T(8,128)(2,1)}, u32[]{:S(2)}) copy-start(bf16[768,3072]{1,0:T(8,128)(2,1)} %all-gather.16.cloned.1.call-done) | copy-start | bytes 14155780
  464.0 10.7 copy-start.16
  464.0 10.7 copy-start.25
  673.6 152.0 %reduce-scatter.11.cloned.1.call-start = ((), (), s32[]{:S(2)}) async-start(), calls=%async_computation.12 | async-start | bytes 5308416 | tf_op jit(solution)/shard_map/reduce_scatter | solution.py:395
  770.4 9.4 copy-start.91
  770.4 256.2 %all-reduce.15.cloned.1.call-start = ((), (), s32[]{:S(2)}) async-start(), calls=%async_computation.13 | async-start | bytes 3145728 | tf_op jit(solution)/shard_map/psum | solution.py:397
  791.6 33.9 %copy-start.55 = (f32[21,128]{1,0:T(8,128)S(1)}, f32[21,128]{1,0:T(8,128)}, u32[]{:S(2)}) copy-start(f32[21,128]{1,0:T(8,128)} %copy-done.54) | copy-start | bytes 32260
  830.5 225.6 %reduce-scatter.7.cloned.1.call-start = ((), (), s32[]{:S(2)}) async-start(), calls=%async_computation.10 | async-start | bytes 19464192 | tf_op jit(solution)/shard_map/reduce_scatter | solution.py:350
  846.0 354.9 %reduce-scatter.9.cloned.1.call-start = ((), (), s32[]{:S(2)}) async-start(), calls=%async_computation.11 | async-start | bytes 9732096 | tf_op jit(solution)/shard_map/reduce_scatter | solution.py:301
  857.3 343.6 %all-reduce.17.cloned.1.call-start = ((), (), s32[]{:S(2)}) async-start(), calls=%async_computation.15 | async-start | bytes 5636096 | tf_op jit(solution)/shard_map/psum | solution.py:404
  866.8 11.1 copy-start.23
  866.8 13.9 %copy-start.40 = (f32[7,141]{1,0:T(8,128)S(1)}, f32[7,141]{1,0:T(8,128)}, u32[]{:S(2)}) copy-start(f32[7,141]{1,0:T(8,128)} %copy-done.39) | copy-start | bytes 11848
  866.8 13.9 %copy-start.77 = (f32[128]{0:T(128)S(1)}, f32[128]{0:T(128)}, u32[]{:S(2)}) copy-start(f32[128]{0:T(128)} %copy-done.76) | copy-start | bytes 1540
  866.8 15.5 %copy-start.59 = (f32[7,141]{1,0:T(8,128)S(1)}, f32[7,141]{1,0:T(8,128)}, u32[]{:S(2)}) copy-start(f32[7,141]{1,0:T(8,128)} %copy-done.58) | copy-start | bytes 11848
  866.8 15.5 %copy-start.49 = (f32[7,141]{1,0:T(8,128)S(1)}, f32[7,141]{1,0:T(8,128)}, u32[]{:S(2)}) copy-start(f32[7,141]{1,0:T(8,128)} %copy-done.48) | copy-start | bytes 11848
  884.2 15.4 %copy-start.9 = (f32[7,141,128]{2,1,0:T(8,128)S(1)}, f32[7,141,128]{2,1,0:T(8,128)}, u32[]{:S(2)}) copy-start(f32[7,141,128]{2,1,0:T(8,128)} %copy-done.8) | copy-start | bytes 1516036
  884.2 15.4 %copy-start.13 = (f32[7,141,128]{2,1,0:T(8,128)S(1)}, f32[7,141,128]{2,1,0:T(8,128)}, u32[]{:S(2)}) copy-start(f32[7,141,128]{2,1,0:T(8,128)} %copy-done.12) | copy-start | bytes 1516036
  884.2 15.4 %copy-start.34 = (f32[128,2048]{1,0:T(8,128)S(1)}, f32[128,2048]{1,0:T(8,128)}, u32[]{:S(2)}) copy-start(f32[128,2048]{1,0:T(8,128)} %param.47) | copy-start | bytes 3145732
  884.2 15.4 %copy-start.43 = (f32[7,141]{1,0:T(8,128)S(1)}, f32[7,141]{1,0:T(8,128)}, u32[]{:S(2)}) copy-start(f32[7,141]{1,0:T(8,128)} %copy-done.42) | copy-start | bytes 11848
  884.3 15.4 %copy-start.51 = (f32[7,141]{1,0:T(8,128)S(1)}, f32[7,141]{1,0:T(8,128)}, u32[]{:S(2)}) copy-start(f32[7,141]{1,0:T(8,128)} %copy-done.50) | copy-start | bytes 11848
  884.3 15.4 %copy-start.82 = (f32[128]{0:T(128)S(1)}, f32[128]{0:T(128)}, u32[]{:S(2)}) copy-start(f32[128]{0:T(128)} %copy-done.81) | copy-start | bytes 1540
  899.7 8.8 copy-start.5
  899.7 8.8 copy-start.11
  899.7 8.8 copy-start.38
  899.7 8.8 copy-start.53
  899.7 8.8 copy-start.66
  928.5 17.8 %slice-start.2 = ((s8[8257536]{0:T(1024)(128)(4,1)}), s8[4194304]{0:T(1024)(128)(4,1)S(1)}, s32[]{:S(2)}) async-start(s8[8257536]{0:T(1024)(128)(4,1)} %bitcast.335), calls=%async_computation.18 | async-start | bytes 8388608
  929.1 11.4 copy-start.89
  929.1 17.2 %slice-start = ((s8[8257536]{0:T(1024)(128)(4,1)}), s8[4194304]{0:T(1024)(128)(4,1)S(1)}, s32[]{:S(2)}) async-start(s8[8257536]{0:T(1024)(128)(4,1)} %bitcast.333), calls=%async_computation.16 | async-start | bytes 8388608
  936.6 9.7 slice-start.3
  946.3 15.4 %copy-start.99 = (pred[16]{0:T(512)(128)(4,1)S(1)}, pred[16]{0:T(512)(128)(4,1)}, u32[]{:S(2)}) copy-start(pred[16]{0:T(512)(128)(4,1)} %copy-done.98) | copy-start | bytes 52
  1200.9 8.3 copy-start.41
  (55 other events, 250.4 us)
Sparse Core Ops, SparseCore 0:
  69.0 34.3 all-gather.9
  120.5 70.7 reduce-scatter.4
  673.7 68.9 all-gather.19
  770.6 54.9 reduce-scatter.10
  830.6 59.2 all-reduce.14
  961.8 177.8 all-reduce.16
Sparse Core Ops, SparseCore 1:
  123.9 80.5 all-gather.11
  207.4 53.1 all-gather.13
  263.4 62.8 all-gather.15
  329.3 62.2 all-gather.17
  846.1 209.9 reduce-scatter.6
  1062.5 138.3 reduce-scatter.8
where the time goes:
time: 1230 us; the launch traced here: 1220 us
  matrix products  474 us (39%)
  waiting for transfers between devices  283 us (23%)
  local copies, waits for them, and re-layouts  181 us (15%)
  blocking collectives  163 us (13%)
  other arithmetic  97.8 us (8%)
  between operations  17.4 us (1%)
    reduce_scatter x1, waiting for transfers between devices, shards(): lax.psum_scatter(contract_rows(activated, grad_top), ('band', 'tok'), sca...  140 us
    dot_general x40, matrix products, times_transpose(): lax.dot_general(left, right, (((1,), (1,)), ((), ())), preferred_element_...  109 us
    dot_general x28, matrix products, contract_rows(): lax.dot_general(left, right, (((0,), (0,)), ((), ())), preferred_element_...  98.8 us
    all_gather x1, waiting for transfers between devices, shards(): gathered_grad = lax.all_gather(grad_embed[None], 'band', axis=0, tiled=True)  68.8 us
    all_gather x1, blocking collectives, shards(): lax.all_gather(shifts, ('band', 'tok'), axis=1, tiled=True)  42.6 us
    psum x1, blocking collectives, shards(): lax.psum((gen_grads[0], gen_grads[1], gen_grads[2], gen_grads[3], gen_gra...  41.7 us
    unnamed x1, blocking collectives  40.6 us
    all_gather x1, blocking collectives, shards(): lax.all_gather(norm_gains, ('band', 'tok'), axis=1, tiled=True)  37.9 us
  transfers between devices with their start and end apart: 12, of which 5 were waited for; matrix products, arithmetic and copies ran while one was open for 34% of the time, Pallas kernels for 0%

commit v1 on v0

v1 whole, which is shorter than its diff:
```python
import math

import jax
import jax.numpy as jnp
from jax import lax
from jax.experimental import pallas as pl
from jax.experimental.pallas import tpu as pltpu
from jax.sharding import PartitionSpec as P

D = 768
HEADS = 12
HD = 64
FF = 3072
WG = 128
GHEADS = 4
GHD = 32
GFF = 2048
NLAT = 128
PIX = 64
SENSORS = 7
BMAX = 12
CHIP = 256
CAP = 4
FRAME = 1024
ROWS = 1032
RP = 1040
CH = 208
BANDS = 4
SLOTS = BMAX // BANDS
OWN = SENSORS * SLOTS
QX = 96

f32 = jnp.float32
bf16 = jnp.bfloat16
BT = ("band", "tok")
HIGH = lax.Precision.HIGHEST
EPS = 1e-05
MASKED = -1000000000.0
MIB = 2**20


def mm(a, b):
    return lax.dot_general(a, b, (((1,), (0,)), ((), ())), preferred_element_type=f32)


def mm_nt(a, b):
    return lax.dot_general(a, b, (((1,), (1,)), ((), ())), preferred_element_type=f32)


def mm_tn(a, b):
    return lax.dot_general(a, b, (((0,), (0,)), ((), ())), preferred_element_type=f32)


def xmm(a, b, dims=((1,), (0,))):
    return lax.dot_general(a, b, (dims, ((), ())), precision=HIGH, preferred_element_type=f32)


def whole(shape):
    return pl.BlockSpec(shape, lambda *_: (0,) * len(shape))


def like(shape, dtype):
    return jax.ShapeDtypeStruct(shape, dtype)


def params(mib):
    return pltpu.CompilerParams(vmem_limit_bytes=mib * MIB)


def center(x):
    xc = x - jnp.mean(x, axis=1, keepdims=True)
    r = lax.rsqrt(jnp.mean(xc * xc, axis=1, keepdims=True) + EPS)
    return xc * r, r


def gelu_parts(u):
    phi = 0.5 + 0.5 * lax.erf(u * math.sqrt(0.5))
    slope = phi + u * (math.sqrt(0.5 / math.pi) * jnp.exp(-0.5 * u * u))
    return u * phi, slope


def col8(v):
    return jnp.sum(v.reshape(v.shape[0] // 8, 8, v.shape[1]), axis=0)


def total(v):
    return jnp.sum(v, axis=0, keepdims=True)


def head_lanes(h):
    lane = lax.broadcasted_iota(jnp.int32, (1, WG), 1)
    return (lane // GHD == h).astype(f32)


def gen_forward(x, latent, bias, w_qkv, w_out, ff1, ff2, gains, shifts):
    scale = 1.0 / math.sqrt(GHD)
    qkv = xmm(x, w_qkv)
    kv = xmm(latent, w_qkv[:, WG:])
    q = qkv[:, :WG] * scale
    k = jnp.concatenate([kv[:, :WG], qkv[:, WG : 2 * WG]], axis=0)
    v = jnp.concatenate([kv[:, WG:], qkv[:, 2 * WG :]], axis=0)
    mixed = jnp.zeros((QX, WG), f32)
    probs = []
    for h in range(GHEADS):
        lanes = head_lanes(h)
        s = xmm(q * lanes, k, ((1,), (1,))) + bias
        e = jnp.exp(s - jnp.max(s, axis=1, keepdims=True))
        p = e / jnp.sum(e, axis=1, keepdims=True)
        probs.append(p)
        mixed = mixed + xmm(p, v * lanes)
    hat1, r1 = center(x + xmm(mixed, w_out))
    z1 = hat1 * gains[0:1] + shifts[0:1]
    act, slope = gelu_parts(xmm(z1, ff1))
    hat2, r2 = center(z1 + xmm(act, ff2))
    z2 = hat2 * gains[1:2] + shifts[1:2]
    return z2, (q, k, v, probs, mixed, hat1, r1, z1, act, slope, hat2, r2)


def gen_fwd_kernel(x, latent, bias, w_qkv, w_out, ff1, ff2, gains, shifts, fc_bias, z2_o, bias_o):
    z2, _ = gen_forward(
        x[...], latent[...], bias[...], w_qkv[...], w_out[...], ff1[...], ff2[...], gains[...], shifts[...]
    )
    z2_o[...] = z2
    bias_o[...] = xmm(z2[QX - 8 :], fc_bias[...])


def gen_fwd(x, latent, bias, w_qkv, w_out, ff1, ff2, gains, shifts, fc_bias):
    args = (x, latent, bias, w_qkv, w_out, ff1, ff2, gains, shifts, fc_bias)
    return pl.pallas_call(
        gen_fwd_kernel,
        in_specs=[whole(a.shape) for a in args],
        out_specs=[whole((QX, WG)), whole((8, D))],
        out_shape=[like((QX, WG), f32), like((8, D), f32)],
        compiler_params=params(40),
        name="gen_fwd",
    )(*args)


def norm_back(g, hat, r, gain):
    s = g * gain
    return r * (s - jnp.mean(s, axis=1, keepdims=True) - hat * jnp.mean(s * hat, axis=1, keepdims=True))


def gen_bwd_kernel(
    x, latent, bias, w_qkv, w_out, ff1, ff2, gains, shifts, fc_bias, dh, dbias,
    dqkv_o, dout_o, dff1_o, dff2_o, dgains_o, dshifts_o, dlat_o, dtok_o, dfcb_o,
):
    scale = 1.0 / math.sqrt(GHD)
    xv, lat, gainv = x[...], latent[...], gains[...]
    z2, (q, k, v, probs, mixed, hat1, r1, z1, act, slope, hat2, r2) = gen_forward(
        xv, lat, bias[...], w_qkv[...], w_out[...], ff1[...], ff2[...], gainv, shifts[...]
    )
    db = dbias[...]
    dfcb_o[...] = xmm(z2[QX - 8 :], db, ((0,), (0,)))
    dz2 = jnp.concatenate([dh[...], xmm(db, fc_bias[...], ((1,), (1,)))], axis=0)
    dw2 = norm_back(dz2, hat2, r2, gainv[1:2])
    dff2_o[...] = xmm(act, dw2, ((0,), (0,)))
    du = xmm(dw2, ff2[...], ((1,), (1,))) * slope
    dff1_o[...] = xmm(z1, du, ((0,), (0,)))
    dz1 = dw2 + xmm(du, ff1[...], ((1,), (1,)))
    dw1 = norm_back(dz1, hat1, r1, gainv[0:1])
    dgains_o[...] = jnp.concatenate([total(dz1 * hat1), total(dz2 * hat2)], axis=0)
    dshifts_o[...] = jnp.concatenate([total(dz1), total(dz2)], axis=0)
    dout_o[...] = xmm(mixed, dw1, ((0,), (0,)))
    dmix = xmm(dw1, w_out[...], ((1,), (1,)))
    dq = jnp.zeros((QX, WG), f32)
    dk = jnp.zeros((NLAT + QX, WG), f32)
    dv = jnp.zeros((NLAT + QX, WG), f32)
    for h in range(GHEADS):
        lanes = head_lanes(h)
        p = probs[h]
        dm = dmix * lanes
        dp = xmm(dm, v, ((1,), (1,)))
        ds = p * (dp - jnp.sum(p * dp, axis=1, keepdims=True))
        dv = dv + xmm(p, dm, ((0,), (0,)))
        dq = dq + xmm(ds, k * lanes)
        dk = dk + xmm(ds, q * lanes, ((0,), (0,)))
    dq = dq * scale
    dx = jnp.concatenate([dq, dk[NLAT:], dv[NLAT:]], axis=1)
    dl = jnp.concatenate([dk[:NLAT], dv[:NLAT]], axis=1)
    wv = w_qkv[...]
    from_x = xmm(xv, dx, ((0,), (0,)))
    from_l = xmm(lat, dl, ((0,), (0,)))
    dqkv_o[:, :WG] = from_x[:, :WG]
    dqkv_o[:, WG:] = from_x[:, WG:] + from_l
    dlat_o[...] = xmm(dl, wv[:, WG:], ((1,), (1,)))
    dx_full = dw1 + xmm(dx, wv, ((1,), (1,)))
    dtok_o[...] = total(dx_full[QX - 8 : QX - 8 + SENSORS])


def gen_bwd(x, latent, bias, w_qkv, w_out, ff1, ff2, gains, shifts, fc_bias, dh, dbias):
    args = (x, latent, bias, w_qkv, w_out, ff1, ff2, gains, shifts, fc_bias, dh, dbias)
    shapes = [(WG, 3 * WG), (WG, WG), (WG, GFF), (GFF, WG), (2, WG), (2, WG), (NLAT, WG), (1, WG), (WG, D)]
    return pl.pallas_call(
        gen_bwd_kernel,
        in_specs=[whole(a.shape) for a in args],
        out_specs=[whole(s) for s in shapes],
        out_shape=[like(s, f32) for s in shapes],
        compiler_params=params(48),
        name="gen_bwd",
    )(*args)


def embed_kernel(sens, pix, kmat, bias, extra, gains, shifts, x0_o, n1_o):
    c = pl.program_id(0)
    rows = pl.ds(c * CHIP, CHIP)
    row = bias[pl.ds(sens[c], 1), :]
    x = mm_tn(pix[...], kmat[0]) + row
    x0_o[rows, :] = x
    hat, _ = center(x)
    n1_o[rows, :] = (hat * gains[0:1] + shifts[0:1]).astype(bf16)

    @pl.when(c == CAP - 1)
    def _():
        e = extra[...]
        x0_o[FRAME:, :] = e
        h, _ = center(e)
        n1_o[FRAME:, :] = (h * gains[0:1] + shifts[0:1]).astype(bf16)


def embed(sens, pix, kmat, bias, extra, gains, shifts):
    return pl.pallas_call(
        embed_kernel,
        grid_spec=pltpu.PrefetchScalarGridSpec(
            num_scalar_prefetch=1,
            grid=(CAP,),
            in_specs=[
                pl.BlockSpec((D, CHIP), lambda c, s: (0, c)),
                pl.BlockSpec((1, D, D), lambda c, s: (s[c], 0, 0)),
                whole((8, D)),
                whole((RP - FRAME, D)),
                whole((8, D)),
                whole((8, D)),
            ],
            out_specs=[whole((RP, D)), whole((RP, D))],
        ),
        out_shape=[like((RP, D), f32), like((RP, D), bf16)],
        compiler_params=params(40),
        name="embed",
    )(sens, pix, kmat, bias, extra, gains, shifts)


def pixel_grad_kernel(sens, band, de, kmat, pix, dpix_o, dker_o, acc):
    n = pl.program_id(0)
    g = de[0]
    dpix_o[0] = mm_nt(kmat[0], g)

    @pl.when(n == 0)
    def _():
        acc[...] = jnp.zeros_like(acc)

    s = sens[n]
    acc[s] = acc[s] + mm(pix[0], g)

    @pl.when(n == pl.num_programs(0) - 1)
    def _():
        dker_o[...] = acc[...]


def pixel_grad(sens, band, de, kmat, pix):
    blocks = BANDS * CAP
    width = SLOTS * PIX
    return pl.pallas_call(
        pixel_grad_kernel,
        grid_spec=pltpu.PrefetchScalarGridSpec(
            num_scalar_prefetch=2,
            grid=(blocks,),
            in_specs=[
                pl.BlockSpec((1, CHIP, D), lambda n, s, b: (n, 0, 0)),
                pl.BlockSpec((1, width, D), lambda n, s, b: (s[n], b[0], 0)),
                pl.BlockSpec((1, width, CHIP), lambda n, s, b: (n // CAP, 0, n % CAP)),
            ],
            out_specs=[
                pl.BlockSpec((1, width, CHIP), lambda n, s, b: (n // CAP, 0, n % CAP)),
                whole((SENSORS, width, D)),
            ],
            scratch_shapes=[pltpu.VMEM((SENSORS, width, D), f32)],
        ),
        out_shape=[like((BANDS, width, FRAME), f32), like((SENSORS, width, D), f32)],
        compiler_params=params(40),
        name="pixel_grad",
    )(sens, band, de, kmat, pix)


GH = 4
GW = GH * HD
GROUPS = HEADS // GH


def attn_fwd_kernel(n1, wq, wk, wv, wo, x0, qa, ka, gains, shifts, q_o, k_o, v_o, o_o, p_o, x1_o, n2_o):
    g = pl.program_id(0)

    @pl.when(g == 0)
    def _():
        x1_o[...] = x0[...]

    for c in range(RP // CH):
        s = pl.ds(c * CH, CH)
        q_o[s, :] = mm(n1[s, :], wq[...]).astype(bf16)
        k_o[s, :] = mm(n1[s, :], wk[...]).astype(bf16)
        v_o[s, :] = mm(n1[s, :], wv[...]).astype(bf16)
    qav = qa[...]
    kav = ka[...]
    for h in range(GH):
        hs = slice(h * HD, (h + 1) * HD)
        kh = jnp.concatenate([k_o[:, hs], kav], axis=1)
        vh = v_o[:, hs]
        for c in range(RP // CH):
            s = pl.ds(c * CH, CH)
            qh = jnp.concatenate([q_o[s, hs] * jnp.bfloat16(0.125), qav[c * CH : (c + 1) * CH]], axis=1)
            sc = mm_nt(qh, kh)
            e = jnp.exp(sc - jnp.max(sc, axis=1, keepdims=True))
            p = (e * (1.0 / jnp.sum(e, axis=1, keepdims=True))).astype(bf16)
            p_o[h, s, :] = p
            o_o[s, hs] = mm(p, vh).astype(bf16)
    for c in range(RP // CH):
        s = pl.ds(c * CH, CH)
        x1_o[s, :] += mm(o_o[s, :], wo[...])

    @pl.when(g == pl.num_programs(0) - 1)
    def _():
        for c in range(RP // CH):
            s = pl.ds(c * CH, CH)
            hat, _ = center(x1_o[s, :])
            n2_o[s, :] = (hat * gains[1:2, :] + shifts[1:2, :]).astype(bf16)


def attn_fwd(n1, w_qkv, w_out, x0, qa, ka, gains, shifts):
    G = GROUPS
    return pl.pallas_call(
        attn_fwd_kernel,
        grid=(G,),
        in_specs=[
            whole((RP, D)),
            pl.BlockSpec((D, GW), lambda g: (0, g)),
            pl.BlockSpec((D, GW), lambda g: (0, G + g)),
            pl.BlockSpec((D, GW), lambda g: (0, 2 * G + g)),
            pl.BlockSpec((GW, D), lambda g: (g, 0)),
            whole((RP, D)),
            whole((RP, HD)),
            whole((RP, HD)),
            whole((8, D)),
            whole((8, D)),
        ],
        out_specs=[pl.BlockSpec((RP, GW), lambda g: (0, g))] * 4
        + [pl.BlockSpec((GH, RP, RP), lambda g: (g, 0, 0)), whole((RP, D)), whole((RP, D))],
        out_shape=[like((RP, D), bf16)] * 4
        + [like((HEADS, RP, RP), bf16), like((RP, D), f32), like((RP, D), bf16)],
        compiler_params=params(60),
        name="attn_fwd",
    )(n1, w_qkv, w_qkv, w_qkv, w_out, x0, qa, ka, gains, shifts)


def attn_bwd_kernel(
    dx1b, wo, q, k, v, o, p, wq, wk, wv, n1, x0, dx1, gains,
    dwo, dwq, dwk, dwv, de_o, tail_o, small_o, dn1_s, do_s, dq_s, dk_s, dv_s, ds_s,
):
    g = pl.program_id(0)

    @pl.when(g == 0)
    def _():
        dn1_s[...] = jnp.zeros_like(dn1_s)

    for c in range(RP // CH):
        s = pl.ds(c * CH, CH)
        do_s[s, :] = mm_nt(dx1b[s, :], wo[...]).astype(bf16)
    dwo[...] = mm_tn(o[...], dx1b[...]).astype(bf16)
    for h in range(GH):
        hs = slice(h * HD, (h + 1) * HD)
        vh = v[:, hs]
        kh = k[:, hs]
        qh = q[:, hs]
        doh = do_s[:, hs]
        for c in range(RP // CH):
            s = pl.ds(c * CH, CH)
            dc = do_s[s, hs]
            inner = jnp.sum(dc.astype(f32) * o[s, hs].astype(f32), axis=1, keepdims=True)
            ds = (p[h, s, :].astype(f32) * (mm_nt(dc, vh) - inner)).astype(bf16)
            ds_s[s, :] = ds
            dq_s[s, hs] = (mm(ds, kh) * 0.125).astype(bf16)
        dk_s[:, hs] = (mm_tn(ds_s[...], qh) * 0.125).astype(bf16)
        dv_s[:, hs] = mm_tn(p[h], doh).astype(bf16)
    for c in range(RP // CH):
        s = pl.ds(c * CH, CH)
        dn1_s[s, :] += mm_nt(dq_s[s, :], wq[...]) + mm_nt(dk_s[s, :], wk[...]) + mm_nt(dv_s[s, :], wv[...])
    dwq[...] = mm_tn(n1[...], dq_s[...]).astype(bf16)
    dwk[...] = mm_tn(n1[...], dk_s[...]).astype(bf16)
    dwv[...] = mm_tn(n1[...], dv_s[...]).astype(bf16)

    @pl.when(g == pl.num_programs(0) - 1)
    def _():
        gg = jnp.zeros((8, D), f32)
        gs = jnp.zeros((8, D), f32)
        for c in range(RP // CH):
            s = pl.ds(c * CH, CH)
            hat, r = center(x0[s, :])
            gr = dn1_s[s, :]
            gg = gg + col8(gr * hat)
            gs = gs + col8(gr)
            dn1_s[s, :] = dx1[s, :] + norm_back(gr, hat, r, gains[0:1, :])
        de_o[...] = dn1_s[:FRAME, :].astype(bf16)
        tail_o[...] = dn1_s[FRAME:, :]
        small_o[0:1, :] = total(gg)
        small_o[1:2, :] = total(gs)
        small_o[2:8, :] = jnp.zeros((6, D), f32)


def attn_bwd(dx1b, w_out, q, k, v, o, p, w_qkv, n1, x0, dx1, gains):
    G = GROUPS
    col = pl.BlockSpec((RP, GW), lambda g: (0, g))
    return pl.pallas_call(
        attn_bwd_kernel,
        grid=(G,),
        in_specs=[
            whole((RP, D)),
            pl.BlockSpec((GW, D), lambda g: (g, 0)),
            col,
            col,
            col,
            col,
            pl.BlockSpec((GH, RP, RP), lambda g: (g, 0, 0)),
            pl.BlockSpec((D, GW), lambda g: (0, g)),
            pl.BlockSpec((D, GW), lambda g: (0, G + g)),
            pl.BlockSpec((D, GW), lambda g: (0, 2 * G + g)),
            whole((RP, D)),
            whole((RP, D)),
            whole((RP, D)),
            whole((8, D)),
        ],
        out_specs=[pl.BlockSpec((GW, D), lambda g: (g, 0))]
        + [pl.BlockSpec((D, GW), lambda g: (0, g))] * 3
        + [whole((FRAME, D)), whole((RP - FRAME, D)), whole((8, D))],
        out_shape=[like((D, D), bf16)] * 4
        + [like((FRAME, D), bf16), like((RP - FRAME, D), f32), like((8, D), f32)],
        scratch_shapes=[pltpu.VMEM((RP, D), f32)]
        + [pltpu.VMEM((RP, GW), bf16)] * 4
        + [pltpu.VMEM((RP, RP), bf16)],
        compiler_params=params(62),
        name="attn_bwd",
    )(dx1b, w_out, q, k, v, o, p, w_qkv, w_qkv, w_qkv, n1, x0, dx1, gains)


FB = 512


def ffn_kernel(
    n2, dout, x1, wup, bup, wdown, gains, shifts,
    out, dwup, dwdown, dbup, dx1_o, dx1b_o, small_o, act_s, du_s, dn2_s, out_s,
):
    j = pl.program_id(0)

    @pl.when(j == 0)
    def _():
        out_s[...] = x1[...] + shifts[2:3, :]
        dn2_s[...] = jnp.zeros_like(dn2_s)

    cs = jnp.zeros((8, FB), f32)
    for c in range(RP // CH):
        s = pl.ds(c * CH, CH)
        u = mm(n2[s, :], wup[...]) + bup[...]
        da = mm_nt(dout[s, :], wdown[...]).astype(bf16).astype(f32)
        act, slope = gelu_parts(u)
        act = act.astype(bf16)
        act_s[s, :] = act
        du = (da * slope).astype(bf16)
        du_s[s, :] = du
        cs = cs + col8(du.astype(f32))
        out_s[s, :] += mm(act, wdown[...])
        dn2_s[s, :] += mm_nt(du, wup[...])
    dbup[...] = jnp.broadcast_to(total(cs), (8, FB))
    dwup[...] = mm_tn(n2[...], du_s[...]).astype(bf16)
    dwdown[...] = mm_tn(act_s[...], dout[...]).astype(bf16)

    @pl.when(j == pl.num_programs(0) - 1)
    def _():
        out[...] = out_s[:ROWS, :]
        gg = jnp.zeros((8, D), f32)
        gs = jnp.zeros((8, D), f32)
        gd = jnp.zeros((8, D), f32)
        for c in range(RP // CH):
            s = pl.ds(c * CH, CH)
            hat, r = center(x1[s, :])
            g = dn2_s[s, :]
            do = dout[s, :].astype(f32)
            gg = gg + col8(g * hat)
            gs = gs + col8(g)
            gd = gd + col8(do)
            dx1 = do + norm_back(g, hat, r, gains[1:2, :])
            dx1_o[s, :] = dx1
            dx1b_o[s, :] = dx1.astype(bf16)
        small_o[0:1, :] = total(gg)
        small_o[1:2, :] = total(gs)
        small_o[2:3, :] = total(gd)
        small_o[3:8, :] = jnp.zeros((5, D), f32)


def ffn(n2, dout, x1, w_up, b_up, w_down, gains, shifts):
    return pl.pallas_call(
        ffn_kernel,
        grid=(FF // FB,),
        in_specs=[
            whole((RP, D)),
            whole((RP, D)),
            whole((RP, D)),
            pl.BlockSpec((D, FB), lambda g: (0, g)),
            pl.BlockSpec((1, FB), lambda g: (0, g)),
            pl.BlockSpec((FB, D), lambda g: (g, 0)),
            whole((8, D)),
            whole((8, D)),
        ],
        out_specs=[
            whole((ROWS, D)),
            pl.BlockSpec((D, FB), lambda g: (0, g)),
            pl.BlockSpec((FB, D), lambda g: (g, 0)),
            pl.BlockSpec((8, FB), lambda g: (0, g)),
            whole((RP, D)),
            whole((RP, D)),
            whole((8, D)),
        ],
        out_shape=[
            like((ROWS, D), f32),
            like((D, FF), bf16),
            like((FF, D), bf16),
            like((8, FF), f32),
            like((RP, D), f32),
            like((RP, D), bf16),
            like((8, D), f32),
        ],
        scratch_shapes=[pltpu.VMEM((RP, FB), bf16)] * 2 + [pltpu.VMEM((RP, D), f32)] * 2,
        compiler_params=params(60),
        name="ffn",
    )(n2, dout, x1, w_up, b_up, w_down, gains, shifts)


def wave_features(wavelengths, wave_index):
    table_size = wavelengths.shape[0]
    picked = (wave_index[..., None] == jnp.arange(table_size, dtype=jnp.int32)).astype(f32)
    wave_values = jnp.sum(picked * wavelengths, axis=-1)
    half_width = WG // 2
    frequency = 1.0 / 10000.0 ** (jnp.arange(half_width, dtype=f32) / half_width)
    angles = 1000.0 * wave_values[..., None] * frequency
    return jnp.concatenate([jnp.sin(angles), jnp.cos(angles)], axis=-1)


def shards(
    pixels, wavelengths, wave_index, band_counts, sensors, chip_lengths, meta_rows,
    w_qkv, w_out, w_up, b_up, w_down, norm_gains, shifts,
    gen_qkv, gen_out, gen_ff1, gen_ff2, gen_gains, gen_shifts, latent_tokens, bias_token,
    fc_kernel, fc_bias, d_out,
):
    band = lax.axis_index("band")
    tok = lax.axis_index("tok")
    toks = lax.axis_size("tok")
    devices = BANDS * toks
    me = band * toks + tok
    share = D // devices
    ff_share = FF // devices
    pix_share = PIX // toks
    width = SLOTS * PIX

    extras = jnp.concatenate(
        [norm_gains.T, shifts.T, b_up.reshape(share, ff_share // share), jnp.zeros((share, 118), bf16)], axis=1
    )
    gathered = lax.all_gather(jnp.concatenate([w_qkv, w_out, extras, w_up], axis=1), BT, axis=0, tiled=True)
    qkv_all = gathered[:, : 3 * D]
    out_all = gathered[:, 3 * D : 4 * D]
    rest = gathered[:, 4 * D : 4 * D + WG].astype(f32)
    up_all = gathered[:, 4 * D + WG :]
    down_all = lax.all_gather(w_down, BT, axis=0, tiled=True)
    gains = jnp.pad(rest[:, :2].T, ((0, 6), (0, 0)))
    shift_rows = jnp.pad(rest[:, 2:6].T, ((0, 4), (0, 0)))
    bias_up = rest[:, 6:10].reshape(1, FF)

    pix_t = pixels.reshape(BANDS, FRAME, width).transpose(0, 2, 1)
    pix_own = lax.all_to_all(pix_t, "band", 0, 0, tiled=True).reshape(BMAX * PIX, FRAME)

    features = wave_features(wavelengths, wave_index).reshape(SENSORS * BMAX, WG)
    valid = jnp.arange(BMAX, dtype=jnp.int32)[None, :] < band_counts[:, None]
    seq = jnp.concatenate([features, jnp.zeros((4, WG), f32), jnp.broadcast_to(bias_token, (8, WG))], axis=0)
    sensor_ids = jnp.arange(SENSORS, dtype=jnp.int32)
    row_sensor = jnp.concatenate(
        [jnp.repeat(sensor_ids, BMAX), jnp.full((4,), 8, jnp.int32), sensor_ids, jnp.full((1,), 9, jnp.int32)]
    )
    key_ok = jnp.concatenate([valid.reshape(-1), jnp.zeros((4,), jnp.bool_), jnp.ones((8,), jnp.bool_)])
    allowed = (row_sensor[:, None] == row_sensor[None, :]) & key_ok[None, :]
    gen_bias = jnp.concatenate([jnp.zeros((QX, NLAT), f32), jnp.where(allowed, 0.0, MASKED)], axis=1)
    gen_args = (seq, latent_tokens, gen_bias, gen_qkv, gen_out, gen_ff1, gen_ff2, gen_gains, gen_shifts, fc_bias)
    z2, bias_vec = gen_fwd(*gen_args)
    h_all = (z2[: SENSORS * BMAX] + features).reshape(SENSORS, BMAX, WG)
    valid_f = valid.astype(f32)

    h_own = lax.dynamic_slice_in_dim(h_all, band * SLOTS, SLOTS, 1).reshape(OWN, WG)
    valid_own = lax.dynamic_slice_in_dim(valid_f, band * SLOTS, SLOTS, 1).reshape(OWN, 1)
    part = (jnp.dot(h_own, fc_kernel, precision=HIGH) * valid_own).astype(bf16).reshape(OWN, pix_share, D)
    kernels = lax.all_gather(part, BT, axis=0, tiled=False)
    kmat = (
        kernels.reshape(BANDS, toks, SENSORS, SLOTS, pix_share, D)
        .transpose(2, 0, 3, 1, 4, 5)
        .reshape(SENSORS, BMAX * PIX, D)
    )

    ends = jnp.cumsum(chip_lengths.reshape(BANDS, CAP), axis=-1)
    starts = jnp.arange(CAP, dtype=jnp.int32) * CHIP
    block_segment = jnp.sum((ends[:, None, :] <= starts[None, :, None]).astype(jnp.int32), axis=-1)
    block_sensor = jnp.take_along_axis(sensors.reshape(BANDS, CAP), block_segment, axis=1)
    own_ends = lax.dynamic_slice_in_dim(ends, band, 1, 0).reshape(CAP)
    own_sensor = lax.dynamic_slice_in_dim(block_sensor, band, 1, 0).reshape(CAP)
    positions = jnp.arange(FRAME, dtype=jnp.int32)
    patch_segment = jnp.sum((own_ends[None, :] <= positions[:, None]).astype(jnp.int32), axis=-1)
    slot_ids = jnp.arange(CAP, dtype=jnp.int32)
    segment = jnp.concatenate([patch_segment, slot_ids, slot_ids, jnp.full((RP - ROWS,), CAP + 1, jnp.int32)])
    onehot = segment[:, None] == jnp.arange(HD, dtype=jnp.int32)[None, :]
    ka = onehot.astype(bf16)
    qa = jnp.where(onehot, 0.0, -(2.0**30)).astype(bf16)

    extra_rows = jnp.concatenate(
        [
            jnp.broadcast_to(shift_rows[3], (CAP, D)),
            meta_rows.reshape(CAP, D).astype(f32),
            jnp.zeros((RP - ROWS, D), f32),
        ],
        axis=0,
    )
    x0, n1 = embed(own_sensor, pix_own, kmat, bias_vec, extra_rows, gains, shift_rows)
    q, k, v, o, probs, x1, n2 = attn_fwd(n1, qkv_all, out_all, x0, qa, ka, gains, shift_rows)
    dout = jnp.pad(d_out.reshape(ROWS, D), ((0, RP - ROWS), (0, 0)))
    out, d_up, d_down, d_bup, dx1, dx1b, small2 = ffn(n2, dout, x1, up_all, bias_up, down_all, gains, shift_rows)
    ff_grads = jnp.concatenate(
        [
            d_up.reshape(devices, share, 4, D).transpose(0, 2, 1, 3).reshape(devices, 4 * share, D),
            d_down.reshape(devices, ff_share, D),
        ],
        axis=1,
    )
    ff_shard = lax.psum_scatter(ff_grads, BT, scatter_dimension=0, tiled=False).astype(f32)
    d_wo, d_wq, d_wk, d_wv, de, tail_rows, small1 = attn_bwd(
        dx1b, out_all, q, k, v, o, probs, qkv_all, n1, x0, dx1, gains
    )
    proj_shard = lax.psum_scatter(
        jnp.concatenate([d_wq, d_wk, d_wv, d_wo], axis=1), BT, scatter_dimension=0, tiled=True
    ).astype(f32)

    de_all = lax.all_gather(de, "band", axis=0, tiled=False)
    d_pix, d_ker = pixel_grad(
        block_sensor.reshape(-1), band.reshape(1), de_all.reshape(BANDS * CAP, CHIP, D), kmat, pix_t
    )
    d_ker = (d_ker.reshape(OWN, PIX, D) * valid_own[:, :, None]).astype(bf16)
    d_cols = lax.psum_scatter(d_ker, "tok", scatter_dimension=1, tiled=True)
    d_cols_all = lax.all_gather(d_cols, "band", axis=0, tiled=False).astype(f32)
    d_cols_all = (
        d_cols_all.reshape(BANDS, SENSORS, SLOTS, pix_share * D)
        .transpose(1, 0, 2, 3)
        .reshape(SENSORS * BMAX, pix_share * D)
    )
    d_fc = xmm(h_all.reshape(SENSORS * BMAX, WG), d_cols_all, ((0,), (0,)))
    dh = lax.psum(xmm(d_cols_all, fc_kernel, ((1,), (1,))), "tok")

    block_sums = jnp.sum(de.reshape(CAP, CHIP, D).astype(f32), axis=1)
    pick = (own_sensor[None, :] == sensor_ids[:, None]).astype(f32)
    d_bias = jnp.sum(pick[:, :, None] * block_sums[None], axis=1)
    d_class = jnp.sum(tail_rows[:CAP], axis=0, keepdims=True)
    smalls = lax.psum(
        jnp.concatenate(
            [d_bup[0].reshape(4, D), small1[0:1], small2[0:1], small1[1:2], small2[1:3], d_class, d_bias], axis=0
        ),
        BT,
    )
    dbias_full = jnp.pad(smalls[10:17], ((0, 1), (0, 0)))
    g = gen_bwd(*gen_args, jnp.pad(dh, ((0, 4), (0, 0))), dbias_full)
    bup_shard = lax.dynamic_slice_in_dim(smalls[0:4].reshape(FF), me * ff_share, ff_share, 0)
    gains_shard = lax.dynamic_slice_in_dim(smalls[4:6], me * share, share, 1)
    shifts_shard = lax.dynamic_slice_in_dim(smalls[6:10], me * share, share, 1)
    up_shard = ff_shard[: 4 * share].reshape(4, share, D).transpose(1, 0, 2).reshape(share, FF)
    return (
        out.reshape(1, 1, ROWS, D),
        d_pix.transpose(0, 2, 1).reshape(BANDS, 1, FRAME, width),
        tail_rows[CAP : 2 * CAP].reshape(1, 1, CAP, D),
        proj_shard[:, : 3 * D],
        proj_shard[:, 3 * D :],
        up_shard,
        bup_shard,
        ff_shard[4 * share :],
        gains_shard,
        shifts_shard,
        g[0],
        g[1],
        g[2],
        g[3],
        g[4],
        g[5],
        g[6],
        g[7].reshape(WG),
        d_fc,
        g[8],
    )


def solution(mesh):
    both = ("band", "tok")
    placed = (
        P(None, "tok", None, "band"),
        P(),
        P(),
        P(),
        P(None, "tok", None),
        P(None, "tok", None),
        P("band", "tok", None, None),
        P(both, None),
        P(both, None),
        P(both, None),
        P(both),
        P(both, None),
        P(None, both),
        P(None, both),
        P(),
        P(),
        P(),
        P(),
        P(),
        P(),
        P(),
        P(),
        P(None, "tok"),
        P(),
        P("band", "tok", None, None),
    )
    return jax.shard_map(
        shards,
        mesh=mesh,
        in_specs=placed,
        out_specs=(
            P("band", "tok", None, None),
            P(None, "tok", None, "band"),
            P("band", "tok", None, None),
            P(both, None),
            P(both, None),
            P(both, None),
            P(both),
            P(both, None),
            P(None, both),
            P(None, both),
            P(),
            P(),
            P(),
            P(),
            P(),
            P(),
            P(),
            P(),
            P(None, "tok"),
            P(),
        ),
        check_vma=False,
    )
```

time: 1230 us -> 835 us (0.68)
  matrix products: 474 us -> 7.9 us
  Pallas kernels: 0 us -> 206 us
  waiting for transfers between devices: 283 us -> 415 us
  local copies, waits for them, and re-layouts: 181 us -> 78 us
  blocking collectives: 163 us -> 81.4 us
  other arithmetic: 97.8 us -> 16.5 us
    dot_general x125 -> x3, matrix products: 474 us -> 7.9 us  [the longest x2 6.3 us: xmm(): lax.dot_general(a, b, (dims, ((), ())), precision=HIGH, preferred_element...]
    pallas_call x0 -> x7, Pallas kernels: none -> 206 us  [the longest x1 65.9 us: attn_bwd(): pl.pallas_call(attn_bwd_kernel, grid=(G,), in_specs=[whole((RP, D)), pl.B...]
    all_gather x6 -> x4, waiting for transfers between devices: 93.1 us -> 197 us  [the longest x1 77 us: shards(): lax.all_gather(jnp.concatenate([w_qkv, w_out, extras, w_up], axis=1), BT,...]
    all_gather x2 -> x1, blocking collectives: 80.5 us -> 13.4 us  [shards(): d_cols_all = lax.all_gather(d_cols, 'band', axis=0, tiled=False).astype(f32)]
    unnamed x1 -> x0, blocking collectives: 40.6 us -> none
    unnamed x12 -> x8, waiting for transfers between devices: 2.39 us -> 35.2 us
    reduce_sum x28 -> x5, other arithmetic: 31.1 us -> 1.26 us  [the longest x1 0.61 us: shards(): d_class = jnp.sum(tail_rows[:CAP], axis=0, keepdims=True)]
    psum x1 -> x2, blocking collectives: 41.7 us -> 67.9 us  [the longest x1 40.6 us: shards(): lax.psum(jnp.concatenate([d_bup[0].reshape(4, D), small1[0:1], small2[0:1...]
  transfers between devices with their start and end apart: 12 -> 8, of which waited for: 5 -> 6; matrix products, arithmetic and copies ran while one was open for 34% -> 8% of each run, Pallas kernels for 0% -> 9%
where the time goes in v1:
time: 835 us; the launch traced here: 826 us
  waiting for transfers between devices  415 us (50%)
  Pallas kernels  206 us (25%)
  blocking collectives  81.4 us (10%)
  local copies, waits for them, and re-layouts  78 us (9%)
  other arithmetic  16.5 us (2%)
  between operations  15 us (2%)
    reduce_scatter x1, waiting for transfers between devices, shards(): lax.psum_scatter(ff_grads, BT, scatter_dimension=0, tiled=False).astype(f32)  138 us
    all_gather x1, waiting for transfers between devices, shards(): lax.all_gather(jnp.concatenate([w_qkv, w_out, extras, w_up], axis=1), BT,...  77 us
    all_gather x1, waiting for transfers between devices, shards(): kernels = lax.all_gather(part, BT, axis=0, tiled=False)  73.8 us
    pallas_call x1, Pallas kernels, attn_bwd(): pl.pallas_call(attn_bwd_kernel, grid=(G,), in_specs=[whole((RP, D)), pl.B...  65.9 us
    pallas_call x1, Pallas kernels, attn_fwd(): pl.pallas_call(attn_fwd_kernel, grid=(G,), in_specs=[whole((RP, D)), pl.B...  53.4 us
    pallas_call x1, Pallas kernels, ffn(): pl.pallas_call(ffn_kernel, grid=(FF // FB,), in_specs=[whole((RP, D)), wh...  47.5 us
    all_gather x1, waiting for transfers between devices, shards(): de_all = lax.all_gather(de, 'band', axis=0, tiled=False)  46.2 us
    reduce_scatter x1, waiting for transfers between devices, shards(): lax.psum_scatter(jnp.concatenate([d_wq, d_wk, d_wv, d_wo], axis=1), BT, s...  44.9 us
  transfers between devices with their start and end apart: 8, of which 6 were waited for; matrix products, arithmetic and copies ran while one was open for 8% of the time, Pallas kernels for 9%

profile of v1, /device:TPU:0, one launch (start us, length us, event | category | flops | bytes accessed | tf_op | source)
XLA Modules:
  0.0 825.7 jit_solution(12070044376872894784)
XLA Ops:
  7.3 0.8 copy.100
  8.1 0.8 select_reduce_fusion
  9.0 0.7 fusion.8
  11.3 1.2 copy-done.5
  12.6 1.2 copy-done.7
  13.8 1.0 copy-done.9
  14.8 0.9 copy-done.11
  15.7 0.8 copy-done.15
  16.6 0.8 copy-done.17
  18.8 4.6 gen_fwd.1
  24.1 0.8 constant_dynamic-slice_fusion.4
  25.1 1.6 fusion
  26.7 0.7 slice_bitcast_fusion.1
  27.7 0.8 reshape.228
  28.5 1.8 concatenate.39
  30.4 0.7 all-gather.11.cloned.1.call-update
  31.1 5.1 all-to-all-start
  36.7 0.7 gather_fusion
  37.6 1.3 pad.23.dout
  39.1 0.9 fusion.1.ka
  40.0 0.9 select_convert_fusion.qa
  40.9 73.8 %all-gather.7.cloned.1.call-done = bf16[32,21,8,768]{3,2,1,0:T(8,128)(2,1)} async-done(((bf16[1,21,8,768]{3,2,1,0:T(8,128)(2,1)}), bf16[32,21,8,768]{3,2,1,0:T(8,128)(2,1)}) %all-gather.7.cloned.1.call-update) | async-done | bytes 8257552 | tf_op jit(solution)/shard_map/all_gather | solution.py:595
  114.7 7.7 copy.102
  122.4 77.0 %all-gather.9.cloned.1.call-done = bf16[768,6272]{1,0:T(8,128)(2,1)} async-done(((bf16[24,6272]{1,0:T(8,128)(2,1)}), bf16[768,6272]{1,0:T(8,128)(2,1)}) %all-gather.9.cloned.1.call-update) | async-done | bytes 9633808 | tf_op jit(solution)/shard_map/all_gather | solution.py:564
  199.4 0.9 slice.104
  200.8 0.9 reshape.230.bup
  201.8 5.2 embed.1
  207.0 5.8 slice.108.wq.wk.wv
  212.8 2.4 slice.109.wo
  215.2 53.4 %attn_fwd.1 = (bf16[1040,768]{1,0:T(8,128)(2,1)}, bf16[1040,768]{1,0:T(8,128)(2,1)}, bf16[1040,768]{1,0:T(8,128)(2,1)}, bf16[1040,768]{1,0:T(8,128)(2,1)}, bf16[...) custom-call(bf16[1040,768]{1,0:T(8,128)(2,1)} %copy-done.3, ...), custom_call_target="tpu_custom_call" | custom-call | tf_op jit(solution)/shard_map/attn_fwd/pallas_call | solution.py:330
  268.6 4.8 slice.110.wup
  273.3 47.5 %ffn.1 = (f32[1032,768]{1,0:T(8,128)}, bf16[768,3072]{1,0:T(8,128)(2,1)}, bf16[3072,768]{1,0:T(8,128)(2,1)}, f32[8,3072]{1,0:T(8,128)}, f32[1040,768]{1,0:T(8,12...) custom-call(bf16[1040,768]{1,0:T(8,128)(2,1)} %get-tuple-element.60.n2, bf16[1040,768]{1,0:T(8,128)(2,1)} %pad.23.dout, ...), custom_call_target="tpu_custom_call" | custom-call | tf_op jit(solution)/shard_map/ffn/pallas_call | solution.py:498
  320.9 65.9 %attn_bwd.1 = (bf16[768,768]{1,0:T(8,128)(2,1)}, bf16[768,768]{1,0:T(8,128)(2,1)}, bf16[768,768]{1,0:T(8,128)(2,1)}, bf16[768,768]{1,0:T(8,128)(2,1)}, bf16[1024...) custom-call(bf16[1040,768]{1,0:T(8,128)(2,1)} %get-tuple-element.63.dx1b, bf16[768,768]{1,0:T(8,128)(2,1)} %slice.109.wo, ...), custom_call_target="tpu_custom_call" | custom-call | tf_op jit(solution)/shard_map/attn_bwd/pallas_call | solution.py:411
  386.8 5.4 pad_maximum_fusion.1
  392.3 9.9 %reshape.236 = bf16[32,24,4,768]{3,2,1,0:T(4,128)(2,1)} reshape(bf16[768,3072]{1,0:T(8,128)(2,1)} %get-tuple-element.77) | data formatting | bytes 9437184 | tf_op jit(solution)/shard_map/reshape | solution.py:630
  402.3 3.4 copy.107
  406.0 3.9 pad_maximum_fusion
  410.1 46.2 %all-gather.13.cloned.1.call-done = bf16[4096,768]{1,0:T(8,128)(2,1)} async-done(((bf16[1024,768]{1,0:T(8,128)(2,1)}), bf16[4096,768]{1,0:T(8,128)(2,1)}) %all-gather.13.cloned.1.call-update) | async-done | bytes 6291472 | tf_op jit(solution)/shard_map/all_gather | solution.py:643
  456.3 2.8 copy-done.4
  459.1 16.1 %pixel_grad.1 = (f32[4,192,1024]{2,1,0:T(8,128)}, f32[7,192,768]{2,1,0:T(8,128)S(1)}) custom-call(s32[16]{0:T(128)S(1)} %and_select_fusion.1.sens, s32[1]{0:T(128)} %bitcast.18.band, bf16[16,256,768]{2,1,0:T(8,128)(2,1)S(1)} %bitcast.72, bf16[7,768,768]{2,1,0:T(8,128)(2,1)} %bitcast.76, bf16[4,192,1024]{2,1,0:T(8,128)(2,1)} %bitcast.5.pix), custom_call_target="tpu_custom_call" | custom-call | tf_op jit(solution)/shard_map/pixel_grad/pallas_call | solution.py:263
  475.8 1.4 copy.116
  477.2 0.7 slice.94
  478.0 0.7 slice.92
  479.3 0.9 slice_reduce_fusion.1
  480.7 0.8 fusion.10
  481.8 40.6 %psum.14 = f32[17,768]{1,0:T(8,128)S(1)} all-reduce(f32[17,768]{1,0:T(8,128)S(1)} %concatenate.44), channel_id=1, replica_groups=mesh['band'=4,'tok'=8] {'band','tok'}, use_global_device_ids=true, to_apply=%region_9.10 | all-reduce | flops 13056 | bytes 104448 | tf_op jit(solution)/shard_map/psum | solution.py:662
  524.3 44.9 %reduce-scatter.6.cloned.1.call-done = bf16[24,3072]{1,0:T(8,128)(2,1)} async-done(((bf16[768,3072]{1,0:T(8,128)(2,1)}), bf16[24,3072]{1,0:T(8,128)(2,1)}) %reduce-scatter.6.cloned.1.call-update) | async-done | bytes 147472 | tf_op jit(solution)/shard_map/reduce_scatter | solution.py:639
  569.2 1.6 slice.112
  570.8 1.4 slice.113
  572.2 138.4 %reduce-scatter.8.cloned.1.call-done = bf16[1,192,768]{2,1,0:T(8,128)(2,1)} async-done(((bf16[32,192,768]{2,1,0:T(8,128)(2,1)}), bf16[1,192,768]{2,1,0:T(8,128)(2,1)}) %reduce-scatter.8.cloned.1.call-update) | async-done | bytes 294928 | tf_op jit(solution)/shard_map/reduce_scatter | solution.py:635
  710.6 0.9 slice.114
  711.5 0.7 copy.114
  712.2 1.0 convert_element_type.72
  713.2 0.7 slice_bitcast_fusion
  714.0 34.4 %reduce-scatter.10.cloned.1.call-done = bf16[8,16128]{1,0:T(8,128)(2,1)} async-done(((bf16[64,16128]{1,0:T(8,128)(2,1)}), bf16[8,16128]{1,0:T(8,128)(2,1)}) %reduce-scatter.10.cloned.1.call-update) | async-done | bytes 258064
  748.4 1.1 reshape.260
  749.5 13.4 %all-gather.1 = bf16[84,8,768]{2,1,0:T(8,128)(2,1)S(1)} all-gather(bf16[21,8,768]{2,1,0:T(8,128)(2,1)S(1)} %copy.112), channel_id=3, replica_groups=mesh['band'=4,'tok'=8] {'band'}, dimensions={0}, use_global_device_ids=true | all-gather | bytes 1290240 | tf_op jit(solution)/shard_map/all_gather | solution.py:649
  763.0 1.3 reshape.243
  764.3 3.2 copy.109
  767.5 3.8 reshape.244
  771.3 3.2 fusion.12
  774.6 3.1 fusion.13
  777.7 27.4 %psum.15 = f32[84,128]{1,0:T(8,128)S(1)} all-reduce(f32[84,128]{1,0:T(8,128)S(1)} %fusion.12), channel_id=1, replica_groups=mesh['band'=4,'tok'=8] {'tok'}, use_global_device_ids=true, to_apply=%region_11.12 | all-reduce | flops 10752 | bytes 86016 | tf_op jit(solution)/shard_map/psum | solution.py:656
  805.1 13.5 %gen_bwd.1 = (f32[128,384]{1,0:T(8,128)}, f32[128,128]{1,0:T(8,128)}, f32[128,2048]{1,0:T(8,128)}, f32[2048,128]{1,0:T(8,128)}, f32[2,128]{1,0:T(2,128)}, /*inde...) custom-call(f32[96,128]{1,0:T(8,128)S(1)} %pad_maximum_fusion.2.x, ...), custom_call_target="tpu_custom_call" | custom-call | tf_op jit(solution)/shard_map/gen_bwd/pallas_call | solution.py:194
  (157 shorter events, 10.2 us)
Async XLA Ops:
  7.2 29.5 %copy-start = (s32[4,1,4]{2,1,0:T(1,128)S(1)}, s32[4,1,4]{2,1,0:T(1,128)}, u32[]{:S(2)}) copy-start(s32[4,1,4]{2,1,0:T(1,128)} %param.29) | copy-start | bytes 196
  7.2 107.5 %all-gather.7.cloned.1.call-start = ((), (), s32[]{:S(2)}) async-start(), calls=%async_computation.4 | async-start | bytes 8515584 | tf_op jit(solution)/shard_map/all_gather | solution.py:595
  11.3 1.2 copy-start.5
  12.6 1.2 copy-start.7
  13.8 1.0 copy-start.9
  14.8 0.9 copy-start.11
  15.7 0.8 copy-start.15
  16.6 0.8 copy-start.17
  17.4 0.7 copy-start.19
  18.1 0.7 copy-start.21
  18.8 6.3 copy-start.23
  23.3 4.2 copy-start.33
  23.3 4.3 copy-start.32
  23.3 5.2 copy-start.28
  26.6 9.6 %copy-start.31 = (s32[4,1,4]{2,1,0:T(1,128)S(1)}, s32[4,1,4]{2,1,0:T(1,128)}, u32[]{:S(2)}) copy-start(s32[4,1,4]{2,1,0:T(1,128)} %param.30) | copy-start | bytes 196
  27.5 172.0 %all-gather.9.cloned.1.call-start = ((), (), s32[]{:S(2)}) async-start(), calls=%async_computation.5 | async-start | bytes 9934848 | tf_op jit(solution)/shard_map/all_gather | solution.py:564
  28.5 9.1 %copy-start.27 = (bf16[1,1,1032,768]{3,2,1,0:T(8,128)(2,1)S(1)}, bf16[1,1,1032,768]{3,2,1,0:T(8,128)(2,1)}, u32[]{:S(2)}) copy-start(bf16[1,1,1032,768]{3,2,1,0:T(8,128)(2,1)} %param.49) | copy-start | bytes 4755460
  30.4 243.0 %all-gather.11.cloned.1.call-start = ((), (), s32[]{:S(2)}) async-start(), calls=%async_computation.6 | async-start | bytes 4866048 | tf_op jit(solution)/shard_map/all_gather | solution.py:569
  31.1 170.7 %all-to-all-start = ((bf16[4,192,1024]{2,1,0:T(8,128)(2,1)}), bf16[4,192,1024]{2,1,0:T(8,128)(2,1)S(1)}, u32[]{:S(2)}, u32[]{:S(2)}) async-start(bf16[4,192,1024]{2,1,0:T(8,128)(2,1)} %bitcast.5.pix), calls=%async_computation | async-start | bytes 3145728 | tf_op jit(solution)/shard_map/all_to_all | solution.py:575
  36.2 2.8 copy-start.30
  36.2 420.1 %all-gather.13.cloned.1.call-start = ((), (), s32[]{:S(2)}) async-start(), calls=%async_computation.9 | async-start | bytes 7864320 | tf_op jit(solution)/shard_map/all_gather | solution.py:643
  200.6 6.4 copy-start.14
  200.6 6.3 copy-start.13
  207.0 5.8 copy-start.2
  207.0 5.8 copy-start.3
  386.8 182.5 %reduce-scatter.6.cloned.1.call-start = ((), (), s32[]{:S(2)}) async-start(), calls=%async_computation.7 | async-start | bytes 4866048 | tf_op jit(solution)/shard_map/reduce_scatter | solution.py:639
  392.3 318.3 %reduce-scatter.8.cloned.1.call-start = ((), (), s32[]{:S(2)}) async-start(), calls=%async_computation.8 | async-start | bytes 9732096 | tf_op jit(solution)/shard_map/reduce_scatter | solution.py:635
  402.3 3.6 slice-start
  402.3 3.7 slice-start.1
  409.9 338.4 %reduce-scatter.10.cloned.1.call-start = ((), (), s32[]{:S(2)}) async-start(), calls=%async_computation.10 | async-start | bytes 2322432
  456.3 2.8 copy-start.4
  475.7 3.0 copy-start.29
  475.7 4.5 copy-start.26
  764.3 7.0 copy-start.24
  771.3 3.2 copy-start.25
  771.3 47.4 %copy-start.1 = (s32[4,1,4]{2,1,0:T(1,128)S(1)}, s32[4,1,4]{2,1,0:T(1,128)}, u32[]{:S(2)}) copy-start(s32[4,1,4]{2,1,0:T(1,128)} %param.29) | copy-start | bytes 196
  774.5 30.6 %copy-start.6 = (f32[128,2048]{1,0:T(8,128)S(1)}, f32[128,2048]{1,0:T(8,128)}, u32[]{:S(2)}) copy-start(f32[128,2048]{1,0:T(8,128)} %ff1.3) | copy-start | bytes 3145732
  774.5 30.6 %copy-start.8 = (f32[2048,128]{1,0:T(8,128)S(1)}, f32[2048,128]{1,0:T(8,128)}, u32[]{:S(2)}) copy-start(f32[2048,128]{1,0:T(8,128)} %ff2.3) | copy-start | bytes 3145732
  774.5 30.6 %copy-start.10 = (f32[128,768]{1,0:T(8,128)S(1)}, f32[128,768]{1,0:T(8,128)}, u32[]{:S(2)}) copy-start(f32[128,768]{1,0:T(8,128)} %fc_bias.3) | copy-start | bytes 1179652
  774.5 30.6 %copy-start.12 = (f32[128,384]{1,0:T(8,128)S(1)}, f32[128,384]{1,0:T(8,128)}, u32[]{:S(2)}) copy-start(f32[128,384]{1,0:T(8,128)} %w_qkv.3) | copy-start | bytes 589828
  774.5 30.6 %copy-start.16 = (f32[128,128]{1,0:T(8,128)S(1)}, f32[128,128]{1,0:T(8,128)}, u32[]{:S(2)}) copy-start(f32[128,128]{1,0:T(8,128)} %latent.3) | copy-start | bytes 196612
  774.5 30.6 %copy-start.18 = (f32[128,128]{1,0:T(8,128)S(1)}, f32[128,128]{1,0:T(8,128)}, u32[]{:S(2)}) copy-start(f32[128,128]{1,0:T(8,128)} %w_out.3) | copy-start | bytes 196612
  774.6 30.6 %copy-start.20 = (f32[2,128]{1,0:T(2,128)S(1)}, f32[2,128]{1,0:T(2,128)}, u32[]{:S(2)}) copy-start(f32[2,128]{1,0:T(2,128)} %gains.3) | copy-start | bytes 3076
  774.6 30.6 %copy-start.22 = (f32[2,128]{1,0:T(2,128)S(1)}, f32[2,128]{1,0:T(2,128)}, u32[]{:S(2)}) copy-start(f32[2,128]{1,0:T(2,128)} %shifts.3) | copy-start | bytes 3076
Sparse Core Ops, SparseCore 0:
  27.6 87.0 all-gather.6
  118.1 81.2 all-gather.8
  202.5 62.2 all-gather.10
  386.9 69.3 all-gather.12
  461.6 107.5 reduce-scatter.5
  576.0 134.5 reduce-scatter.7
  713.4 34.8 reduce-scatter.9

commit v2 on v1

--- a/solution.py
+++ b/solution.py
@@ -28,6 +28,7 @@
 BANDS = 4
 SLOTS = BMAX // BANDS
 OWN = SENSORS * SLOTS
+HALF = D // 2
 QX = 96
 
 f32 = jnp.float32
@@ -201,11 +202,20 @@
     )(*args)
 
 
-def embed_kernel(sens, pix, kmat, bias, extra, gains, shifts, x0_o, n1_o):
+def embed_kernel(sens, core, *refs):
+    pix = refs[:BANDS]
+    own = refs[BANDS : 2 * BANDS]
+    other = refs[2 * BANDS : 3 * BANDS]
+    bias, extra, gains, shifts, x0_o, n1_o = refs[3 * BANDS :]
     c = pl.program_id(0)
     rows = pl.ds(c * CHIP, CHIP)
     row = bias[pl.ds(sens[c], 1), :]
-    x = mm_tn(pix[...], kmat[0]) + row
+    for half, ker in ((core[0], own), (1 - core[0], other)):
+        acc = mm_tn(pix[0][...], ker[0][0])
+        for r in range(1, BANDS):
+            acc = acc + mm_tn(pix[r][...], ker[r][0])
+        x0_o[rows, pl.ds(pl.multiple_of(half * HALF, HALF), HALF)] = acc
+    x = x0_o[rows, :] + row
     x0_o[rows, :] = x
     hat, _ = center(x)
     n1_o[rows, :] = (hat * gains[0:1] + shifts[0:1]).astype(bf16)
@@ -218,68 +228,67 @@
         n1_o[FRAME:, :] = (h * gains[0:1] + shifts[0:1]).astype(bf16)
 
 
-def embed(sens, pix, kmat, bias, extra, gains, shifts):
+def embed(sens, core, pix, own, other, bias, extra, gains, shifts):
+    width = SLOTS * PIX
     return pl.pallas_call(
         embed_kernel,
         grid_spec=pltpu.PrefetchScalarGridSpec(
-            num_scalar_prefetch=1,
+            num_scalar_prefetch=2,
             grid=(CAP,),
-            in_specs=[
-                pl.BlockSpec((D, CHIP), lambda c, s: (0, c)),
-                pl.BlockSpec((1, D, D), lambda c, s: (s[c], 0, 0)),
-                whole((8, D)),
-                whole((RP - FRAME, D)),
-                whole((8, D)),
-                whole((8, D)),
-            ],
+            in_specs=[pl.BlockSpec((width, CHIP), lambda c, *_: (0, c))] * BANDS
+            + [pl.BlockSpec((1, width, HALF), lambda c, s, _: (s[c], 0, 0))] * (2 * BANDS)
+            + [whole((8, D)), whole((RP - FRAME, D)), whole((8, D)), whole((8, D))],
             out_specs=[whole((RP, D)), whole((RP, D))],
         ),
         out_shape=[like((RP, D), f32), like((RP, D), bf16)],
         compiler_params=params(40),
+        cost_estimate=pl.CostEstimate(flops=2 * FRAME * D * D, bytes_accessed=14 * MIB, transcendentals=0),
         name="embed",
-    )(sens, pix, kmat, bias, extra, gains, shifts)
-
-
-def pixel_grad_kernel(sens, band, de, kmat, pix, dpix_o, dker_o, acc):
+    )(sens, core, *pix, *own, *other, bias, extra, gains, shifts)
+
+
+def pixel_grad_kernel(first, sens, frames, core, de, k_own, k_oth, pix, *refs):
+    if first:
+        dpix_o, dker_o = refs
+    else:
+        _, before, dpix_o, dker_o = refs
     n = pl.program_id(0)
-    g = de[0]
-    dpix_o[0] = mm_nt(kmat[0], g)
 
     @pl.when(n == 0)
     def _():
-        acc[...] = jnp.zeros_like(acc)
-
+        dker_o[...] = jnp.zeros_like(dker_o) if first else before[...]
+
+    g = de[0]
+    lo = pl.ds(pl.multiple_of(core[0] * HALF, HALF), HALF)
+    hi = pl.ds(pl.multiple_of((1 - core[0]) * HALF, HALF), HALF)
+    dpix_o[0] = mm_nt(k_own[0], de[0, :, lo]) + mm_nt(k_oth[0], de[0, :, hi])
     s = sens[n]
-    acc[s] = acc[s] + mm(pix[0], g)
-
-    @pl.when(n == pl.num_programs(0) - 1)
-    def _():
-        dker_o[...] = acc[...]
-
-
-def pixel_grad(sens, band, de, kmat, pix):
-    blocks = BANDS * CAP
+    dker_o[s] = dker_o[s] + mm(pix[0], g)
+
+
+def pixel_grad(sens, frames, core, de, k_own, k_oth, pix, before):
+    blocks = de.shape[0]
     width = SLOTS * PIX
+    first = not before
+    here = pl.BlockSpec((1, width, CHIP), lambda n, s, f, c: (f[n // CAP], 0, n % CAP))
+    kern = pl.BlockSpec((1, width, HALF), lambda n, s, f, c: (s[n], 0, 0))
+    more = [] if first else [pl.BlockSpec(memory_space=pl.ANY), whole((SENSORS, width, D))]
     return pl.pallas_call(
-        pixel_grad_kernel,
+        lambda *refs: pixel_grad_kernel(first, *refs),
         grid_spec=pltpu.PrefetchScalarGridSpec(
-            num_scalar_prefetch=2,
+            num_scalar_prefetch=3,
             grid=(blocks,),
-            in_specs=[
-                pl.BlockSpec((1, CHIP, D), lambda n, s, b: (n, 0, 0)),
-                pl.BlockSpec((1, width, D), lambda n, s, b: (s[n], b[0], 0)),
-                pl.BlockSpec((1, width, CHIP), lambda n, s, b: (n // CAP, 0, n % CAP)),
-            ],
-            out_specs=[
-                pl.BlockSpec((1, width, CHIP), lambda n, s, b: (n // CAP, 0, n % CAP)),
-                whole((SENSORS, width, D)),
-            ],
-            scratch_shapes=[pltpu.VMEM((SENSORS, width, D), f32)],
+            in_specs=[pl.BlockSpec((1, CHIP, D), lambda n, s, f, c: (n, 0, 0)), kern, kern, here] + more,
+            out_specs=[here, whole((SENSORS, width, D))],
         ),
         out_shape=[like((BANDS, width, FRAME), f32), like((SENSORS, width, D), f32)],
+        input_output_aliases={} if first else {7: 0, 8: 1},
         compiler_params=params(40),
+        cost_estimate=pl.CostEstimate(
+            flops=blocks * 4 * CHIP * D * width, bytes_accessed=blocks * MIB, transcendentals=0
+        ),
         name="pixel_grad",
-    )(sens, band, de, kmat, pix)
+    )(sens, frames, core, de, k_own, k_oth, pix, *before)
 
 
 GH = 4
@@ -325,17 +334,16 @@
             n2_o[s, :] = (hat * gains[1:2, :] + shifts[1:2, :]).astype(bf16)
 
 
-def attn_fwd(n1, w_qkv, w_out, x0, qa, ka, gains, shifts):
-    G = GROUPS
+def attn_fwd(n1, weights, x0, qa, ka, gains, shifts):
     return pl.pallas_call(
         attn_fwd_kernel,
-        grid=(G,),
+        grid=(GROUPS,),
         in_specs=[
             whole((RP, D)),
             pl.BlockSpec((D, GW), lambda g: (0, g)),
-            pl.BlockSpec((D, GW), lambda g: (0, G + g)),
-            pl.BlockSpec((D, GW), lambda g: (0, 2 * G + g)),
-            pl.BlockSpec((GW, D), lambda g: (g, 0)),
+            pl.BlockSpec((D, GW), lambda g: (0, GROUPS + g)),
+            pl.BlockSpec((D, GW), lambda g: (0, 2 * GROUPS + g)),
+            pl.BlockSpec((GW, D), lambda g: (g, 3)),
             whole((RP, D)),
             whole((RP, HD)),
             whole((RP, HD)),
@@ -347,19 +355,23 @@
         out_shape=[like((RP, D), bf16)] * 4
         + [like((HEADS, RP, RP), bf16), like((RP, D), f32), like((RP, D), bf16)],
         compiler_params=params(60),
+        cost_estimate=pl.CostEstimate(flops=5 * 10**10, bytes_accessed=50 * MIB, transcendentals=0),
         name="attn_fwd",
-    )(n1, w_qkv, w_qkv, w_qkv, w_out, x0, qa, ka, gains, shifts)
+    )(n1, weights, weights, weights, weights, x0, qa, ka, gains, shifts)
 
 
 def attn_bwd_kernel(
-    dx1b, wo, q, k, v, o, p, wq, wk, wv, n1, x0, dx1, gains,
-    dwo, dwq, dwk, dwv, de_o, tail_o, small_o, dn1_s, do_s, dq_s, dk_s, dv_s, ds_s,
+    last, dx1b, wo, q, k, v, o, p, wq, wk, wv, n1, before, *refs
 ):
+    if last:
+        x0, dx1, gains, dwo, dwq, dwk, dwv, de_o, tail_o, small_o, dn1_s, do_s, dq_s, dk_s, dv_s, ds_s = refs
+    else:
+        dwo, dwq, dwk, dwv, dn1_s, do_s, dq_s, dk_s, dv_s, ds_s = refs
     g = pl.program_id(0)
 
     @pl.when(g == 0)
     def _():
-        dn1_s[...] = jnp.zeros_like(dn1_s)
+        dn1_s[...] = before[...]
 
     for c in range(RP // CH):
         s = pl.ds(c * CH, CH)
@@ -386,6 +398,8 @@
     dwq[...] = mm_tn(n1[...], dq_s[...]).astype(bf16)
     dwk[...] = mm_tn(n1[...], dk_s[...]).astype(bf16)
     dwv[...] = mm_tn(n1[...], dv_s[...]).astype(bf16)
+    if not last:
+        return
 
     @pl.when(g == pl.num_programs(0) - 1)
     def _():
@@ -405,47 +419,51 @@
         small_o[2:8, :] = jnp.zeros((6, D), f32)
 
 
-def attn_bwd(dx1b, w_out, q, k, v, o, p, w_qkv, n1, x0, dx1, gains):
-    G = GROUPS
-    col = pl.BlockSpec((RP, GW), lambda g: (0, g))
+def attn_bwd(start, count, last, dx1b, weights, q, k, v, o, p, n1, before, ends=()):
+    col = pl.BlockSpec((RP, GW), lambda g: (0, start + g))
+    grads = [like((count * GW, D), bf16)] + [like((D, count * GW), bf16)] * 3
+    grad_specs = [pl.BlockSpec((GW, D), lambda g: (g, 0))] + [pl.BlockSpec((D, GW), lambda g: (0, g))] * 3
+    work = [pltpu.VMEM((RP, GW), bf16)] * 4 + [pltpu.VMEM((RP, RP), bf16)]
+    if last:
+        out_shape = grads + [like((FRAME, D), bf16), like((RP - FRAME, D), f32), like((8, D), f32)]
+        out_specs = grad_specs + [whole((FRAME, D)), whole((RP - FRAME, D)), whole((8, D))]
+        work = [pltpu.VMEM((RP, D), f32)] + work
+    else:
+        out_shape = grads + [like((RP, D), f32)]
+        out_specs = grad_specs + [whole((RP, D))]
     return pl.pallas_call(
-        attn_bwd_kernel,
-        grid=(G,),
+        lambda *refs: attn_bwd_kernel(last, *refs),
+        grid=(count,),
         in_specs=[
             whole((RP, D)),
-            pl.BlockSpec((GW, D), lambda g: (g, 0)),
+            pl.BlockSpec((GW, D), lambda g: (start + g, 3)),
             col,
             col,
             col,
             col,
-            pl.BlockSpec((GH, RP, RP), lambda g: (g, 0, 0)),
-            pl.BlockSpec((D, GW), lambda g: (0, g)),
-            pl.BlockSpec((D, GW), lambda g: (0, G + g)),
-            pl.BlockSpec((D, GW), lambda g: (0, 2 * G + g)),
-            whole((RP, D)),
-            whole((RP, D)),
-            whole((RP, D)),
-            whole((8, D)),
-        ],
-        out_specs=[pl.BlockSpec((GW, D), lambda g: (g, 0))]
-        + [pl.BlockSpec((D, GW), lambda g: (0, g))] * 3
-        + [whole((FRAME, D)), whole((RP - FRAME, D)), whole((8, D))],
-        out_shape=[like((D, D), bf16)] * 4
-        + [like((FRAME, D), bf16), like((RP - FRAME, D), f32), like((8, D), f32)],
-        scratch_shapes=[pltpu.VMEM((RP, D), f32)]
-        + [pltpu.VMEM((RP, GW), bf16)] * 4
-        + [pltpu.VMEM((RP, RP), bf16)],
+            pl.BlockSpec((GH, RP, RP), lambda g: (start + g, 0, 0)),
+            pl.BlockSpec((D, GW), lambda g: (0, start + g)),
+            pl.BlockSpec((D, GW), lambda g: (0, GROUPS + start + g)),
+            pl.BlockSpec((D, GW), lambda g: (0, 2 * GROUPS + start + g)),
+            whole((RP, D)),
+            whole((RP, D)),
+        ]
+        + ([whole((RP, D)), whole((RP, D)), whole((8, D))] if last else []),
+        out_specs=out_specs,
+        out_shape=out_shape,
+        scratch_shapes=work,
         compiler_params=params(62),
+        cost_estimate=pl.CostEstimate(flops=count * 2 * 10**10, bytes_accessed=count * 20 * MIB, transcendentals=0),
         name="attn_bwd",
-    )(dx1b, w_out, q, k, v, o, p, w_qkv, w_qkv, w_qkv, n1, x0, dx1, gains)
-
-
-FB = 512
+    )(dx1b, weights, q, k, v, o, p, weights, weights, weights, n1, before, *ends)
+
+
+FB = 768
 
 
 def ffn_kernel(
     n2, dout, x1, wup, bup, wdown, gains, shifts,
-    out, dwup, dwdown, dbup, dx1_o, dx1b_o, small_o, act_s, du_s, dn2_s, out_s,
+    out, dw, dbup, dx1_o, dx1b_o, small_o, act_s, du_s, dn2_s, out_s,
 ):
     j = pl.program_id(0)
 
@@ -468,8 +486,8 @@
         out_s[s, :] += mm(act, wdown[...])
         dn2_s[s, :] += mm_nt(du, wup[...])
     dbup[...] = jnp.broadcast_to(total(cs), (8, FB))
-    dwup[...] = mm_tn(n2[...], du_s[...]).astype(bf16)
-    dwdown[...] = mm_tn(act_s[...], dout[...]).astype(bf16)
+    dw[:, :FB] = mm_tn(n2[...], du_s[...]).astype(bf16)
+    dw[:, FB:] = mm_tn(act_s[...], dout[...]).astype(bf16)
 
     @pl.when(j == pl.num_programs(0) - 1)
     def _():
@@ -494,7 +512,7 @@
         small_o[3:8, :] = jnp.zeros((5, D), f32)
 
 
-def ffn(n2, dout, x1, w_up, b_up, w_down, gains, shifts):
+def ffn(n2, dout, x1, weights, b_up, gains, shifts):
     return pl.pallas_call(
         ffn_kernel,
         grid=(FF // FB,),
@@ -502,16 +520,15 @@
             whole((RP, D)),
             whole((RP, D)),
             whole((RP, D)),
-            pl.BlockSpec((D, FB), lambda g: (0, g)),
+            pl.BlockSpec((D, FB), lambda g: (0, 4 + g)),
             pl.BlockSpec((1, FB), lambda g: (0, g)),
-            pl.BlockSpec((FB, D), lambda g: (g, 0)),
+            pl.BlockSpec((FB, D), lambda g: (0, 8 + g)),
             whole((8, D)),
             whole((8, D)),
         ],
         out_specs=[
             whole((ROWS, D)),
-            pl.BlockSpec((D, FB), lambda g: (0, g)),
-            pl.BlockSpec((FB, D), lambda g: (g, 0)),
+            pl.BlockSpec((D, 2 * FB), lambda g: (0, g)),
             pl.BlockSpec((8, FB), lambda g: (0, g)),
             whole((RP, D)),
             whole((RP, D)),
@@ -519,17 +536,68 @@
         ],
         out_shape=[
             like((ROWS, D), f32),
-            like((D, FF), bf16),
-            like((FF, D), bf16),
+            like((D, 2 * FF), bf16),
             like((8, FF), f32),
             like((RP, D), f32),
             like((RP, D), bf16),
             like((8, D), f32),
         ],
         scratch_shapes=[pltpu.VMEM((RP, FB), bf16)] * 2 + [pltpu.VMEM((RP, D), f32)] * 2,
-        compiler_params=params(60),
+        compiler_params=params(62),
+        cost_estimate=pl.CostEstimate(flops=45 * 10**9, bytes_accessed=30 * MIB, transcendentals=0),
         name="ffn",
-    )(n2, dout, x1, w_up, b_up, w_down, gains, shifts)
+    )(n2, dout, x1, weights, b_up, weights, gains, shifts)
+
+
+def flip(v, axis, bits):
+    return lax.ppermute(v, axis, [(i, i ^ bits) for i in range(lax.axis_size(axis))])
+
+
+def terms(v, axis, step, count):
+    return [v] + [flip(v, axis, k * step) for k in range(1, count)]
+
+
+def tree_sum(parts):
+    parts = list(parts)
+    while len(parts) > 1:
+        parts = [parts[i] + parts[i + 1] for i in range(0, len(parts), 2)]
+    return parts[0]
+
+
+def in_order(parts, place):
+    parts = list(parts)
+    bit = 1
+    while bit < len(parts):
+        odd = (place & bit) != 0
+        parts = [jnp.where(odd, parts[i ^ bit], parts[i]) for i in range(len(parts))]
+        bit *= 2
+    return parts
+
+
+def pick(v, i, axis=0):
+    return lax.dynamic_index_in_dim(v, i, axis, keepdims=False)
+
+
+def sum_low(parts):
+    return tree_sum([p.astype(f32) for p in parts])
+
+
+def scatter_core(v, core):
+    got = flip(pick(v, 1 - core, 2), "tok", 1)
+    return sum_low([pick(v, core, 2), got]).astype(bf16)
+
+
+def scatter_band(v, band):
+    return sum_low([pick(v, band)] + [flip(pick(v, band ^ r), "band", r) for r in range(1, BANDS)]).astype(bf16)
+
+
+def scatter_z(v, z):
+    return sum_low([pick(v, z)] + [flip(pick(v, z ^ k), "tok", 2 * k) for k in range(1, v.shape[0])])
+
+
+def sum_tok(v, chips):
+    v = v + flip(v, "tok", 1)
+    return tree_sum(terms(v, "tok", 2, chips))
 
 
 def wave_features(wavelengths, wave_index):
@@ -551,6 +619,9 @@
     band = lax.axis_index("band")
     tok = lax.axis_index("tok")
     toks = lax.axis_size("tok")
+    chips = toks // 2
+    core = tok % 2
+    z = tok // 2
     devices = BANDS * toks
     me = band * toks + tok
     share = D // devices
@@ -558,21 +629,25 @@
     pix_share = PIX // toks
     width = SLOTS * PIX
 
-    extras = jnp.concatenate(
-        [norm_gains.T, shifts.T, b_up.reshape(share, ff_share // share), jnp.zeros((share, 118), bf16)], axis=1
-    )
-    gathered = lax.all_gather(jnp.concatenate([w_qkv, w_out, extras, w_up], axis=1), BT, axis=0, tiled=True)
-    qkv_all = gathered[:, : 3 * D]
-    out_all = gathered[:, 3 * D : 4 * D]
-    rest = gathered[:, 4 * D : 4 * D + WG].astype(f32)
-    up_all = gathered[:, 4 * D + WG :]
-    down_all = lax.all_gather(w_down, BT, axis=0, tiled=True)
-    gains = jnp.pad(rest[:, :2].T, ((0, 6), (0, 0)))
-    shift_rows = jnp.pad(rest[:, 2:6].T, ((0, 4), (0, 0)))
-    bias_up = rest[:, 6:10].reshape(1, FF)
-
     pix_t = pixels.reshape(BANDS, FRAME, width).transpose(0, 2, 1)
-    pix_own = lax.all_to_all(pix_t, "band", 0, 0, tiled=True).reshape(BMAX * PIX, FRAME)
+    pix = [pick(pix_t, band)] + [flip(pick(pix_t, band ^ r), "band", r) for r in range(1, BANDS)]
+
+    vectors = jnp.concatenate([norm_gains.T, shifts.T, b_up.reshape(4, share).T], axis=1)
+    weights = jnp.concatenate(
+        [
+            w_qkv,
+            w_out,
+            w_up.reshape(share, devices, 4, share).transpose(0, 2, 1, 3).reshape(share, FF),
+            w_down.reshape(4, share, D).transpose(1, 0, 2).reshape(share, FF),
+            jnp.pad(vectors, ((0, 0), (0, WG - vectors.shape[1]))),
+        ],
+        axis=1,
+    )
+    weights = lax.all_gather(weights, BT, axis=0, tiled=True)
+    rest = weights[:, 12 * D : 12 * D + 10].astype(f32).T
+    gains = jnp.pad(rest[:2], ((0, 6), (0, 0)))
+    shift_rows = jnp.pad(rest[2:6], ((0, 4), (0, 0)))
+    bias_up = rest[6:10].reshape(1, FF)
 
     features = wave_features(wavelengths, wave_index).reshape(SENSORS * BMAX, WG)
     valid = jnp.arange(BMAX, dtype=jnp.int32)[None, :] < band_counts[:, None]
@@ -589,22 +664,12 @@
     h_all = (z2[: SENSORS * BMAX] + features).reshape(SENSORS, BMAX, WG)
     valid_f = valid.astype(f32)
 
-    h_own = lax.dynamic_slice_in_dim(h_all, band * SLOTS, SLOTS, 1).reshape(OWN, WG)
-    valid_own = lax.dynamic_slice_in_dim(valid_f, band * SLOTS, SLOTS, 1).reshape(OWN, 1)
-    part = (jnp.dot(h_own, fc_kernel, precision=HIGH) * valid_own).astype(bf16).reshape(OWN, pix_share, D)
-    kernels = lax.all_gather(part, BT, axis=0, tiled=False)
-    kmat = (
-        kernels.reshape(BANDS, toks, SENSORS, SLOTS, pix_share, D)
-        .transpose(2, 0, 3, 1, 4, 5)
-        .reshape(SENSORS, BMAX * PIX, D)
-    )
-
     ends = jnp.cumsum(chip_lengths.reshape(BANDS, CAP), axis=-1)
     starts = jnp.arange(CAP, dtype=jnp.int32) * CHIP
     block_segment = jnp.sum((ends[:, None, :] <= starts[None, :, None]).astype(jnp.int32), axis=-1)
     block_sensor = jnp.take_along_axis(sensors.reshape(BANDS, CAP), block_segment, axis=1)
-    own_ends = lax.dynamic_slice_in_dim(ends, band, 1, 0).reshape(CAP)
-    own_sensor = lax.dynamic_slice_in_dim(block_sensor, band, 1, 0).reshape(CAP)
+    own_ends = pick(ends, band)
+    frame_sensor = [pick(block_sensor, band ^ r) for r in range(BANDS)]
     positions = jnp.arange(FRAME, dtype=jnp.int32)
     patch_segment = jnp.sum((own_ends[None, :] <= positions[:, None]).astype(jnp.int32), axis=-1)
     slot_ids = jnp.arange(CAP, dtype=jnp.int32)
@@ -613,6 +678,19 @@
     ka = onehot.astype(bf16)
     qa = jnp.where(onehot, 0.0, -(2.0**30)).astype(bf16)
 
+    h_own = lax.dynamic_slice_in_dim(h_all, band * SLOTS, SLOTS, 1).reshape(OWN, WG)
+    valid_own = lax.dynamic_slice_in_dim(valid_f, band * SLOTS, SLOTS, 1).reshape(OWN, 1)
+    part = (jnp.dot(h_own, fc_kernel, precision=HIGH) * valid_own).astype(bf16).reshape(OWN, pix_share, 2, HALF)
+    mine = pick(part, core, 2)
+    got = flip(pick(part, 1 - core, 2), "tok", 1)
+    got, *pix = lax.optimization_barrier((got, *pix))
+    pair = jnp.where(core == 0, jnp.concatenate([mine, got], axis=1), jnp.concatenate([got, mine], axis=1))
+    k_own = jnp.concatenate(in_order(terms(pair, "tok", 2, chips), z), axis=1).reshape(SENSORS, width, HALF)
+
+    ker_own = terms(k_own, "band", 1, BANDS)
+    ker_other = [flip(v, "tok", 1) for v in ker_own]
+    k_other = ker_other[0]
+
     extra_rows = jnp.concatenate(
         [
             jnp.broadcast_to(shift_rows[3], (CAP, D)),
@@ -621,65 +699,83 @@
         ],
         axis=0,
     )
-    x0, n1 = embed(own_sensor, pix_own, kmat, bias_vec, extra_rows, gains, shift_rows)
-    q, k, v, o, probs, x1, n2 = attn_fwd(n1, qkv_all, out_all, x0, qa, ka, gains, shift_rows)
+    which = core.reshape(1)
+    x0, n1 = embed(frame_sensor[0], which, pix, ker_own, ker_other, bias_vec, extra_rows, gains, shift_rows)
+    q, k, v, o, probs, x1, n2 = attn_fwd(n1, weights, x0, qa, ka, gains, shift_rows)
     dout = jnp.pad(d_out.reshape(ROWS, D), ((0, RP - ROWS), (0, 0)))
-    out, d_up, d_down, d_bup, dx1, dx1b, small2 = ffn(n2, dout, x1, up_all, bias_up, down_all, gains, shift_rows)
-    ff_grads = jnp.concatenate(
-        [
-            d_up.reshape(devices, share, 4, D).transpose(0, 2, 1, 3).reshape(devices, 4 * share, D),
-            d_down.reshape(devices, ff_share, D),
-        ],
-        axis=1,
-    )
-    ff_shard = lax.psum_scatter(ff_grads, BT, scatter_dimension=0, tiled=False).astype(f32)
+    out, d_ff, d_bup, dx1, dx1b, small2 = ffn(n2, dout, x1, weights, bias_up, gains, shift_rows)
+    d_ff = lax.psum_scatter(d_ff, BT, scatter_dimension=0, tiled=True).astype(f32).reshape(share, 8, D)
+    args = (dx1b, weights, q, k, v, o, probs, n1)
     d_wo, d_wq, d_wk, d_wv, de, tail_rows, small1 = attn_bwd(
-        dx1b, out_all, q, k, v, o, probs, qkv_all, n1, x0, dx1, gains
-    )
-    proj_shard = lax.psum_scatter(
-        jnp.concatenate([d_wq, d_wk, d_wv, d_wo], axis=1), BT, scatter_dimension=0, tiled=True
-    ).astype(f32)
-
-    de_all = lax.all_gather(de, "band", axis=0, tiled=False)
-    d_pix, d_ker = pixel_grad(
-        block_sensor.reshape(-1), band.reshape(1), de_all.reshape(BANDS * CAP, CHIP, D), kmat, pix_t
-    )
+        0, GROUPS, True, *args, jnp.zeros((RP, D), f32), (x0, dx1, gains)
+    )
+
+    de_x = flip(de, "band", 1)
+    de_y = flip(de, "band", 2)
+    d_proj = jnp.concatenate([d_wq, d_wk, d_wv, d_wo], axis=1).reshape(BANDS, chips, 2, share, 4 * D)
+    d_proj = scatter_core(d_proj, core)
+
+    def grads(group, done):
+        return pixel_grad(
+            jnp.concatenate([frame_sensor[r] for r, _ in group]),
+            jnp.stack([band ^ r for r, _ in group]),
+            which,
+            jnp.concatenate([g.reshape(CAP, CHIP, D) for _, g in group], axis=0),
+            k_own,
+            k_other,
+            pix_t,
+            done,
+        )
+
+    done = grads(((0, de),), ())
+    half = FRAME // 2
+    d_proj, de_x, de_y = lax.optimization_barrier((d_proj, de_x, de_y))
+    de_xy = jnp.concatenate([flip(de_x[:half], "band", 2), flip(de_y[half:], "band", 1)], axis=0)
+    done = grads(((1, de_x), (2, de_y)), done)
+    d_proj, de_xy = lax.optimization_barrier((d_proj, de_xy))
+    d_proj = scatter_band(d_proj, band)
+    done = grads(((3, de_xy),), done)
+    d_pix, d_ker = done
     d_ker = (d_ker.reshape(OWN, PIX, D) * valid_own[:, :, None]).astype(bf16)
-    d_cols = lax.psum_scatter(d_ker, "tok", scatter_dimension=1, tiled=True)
-    d_cols_all = lax.all_gather(d_cols, "band", axis=0, tiled=False).astype(f32)
+    d_ker = scatter_core(d_ker.reshape(1, OWN * chips, 2, pix_share, D), core)
+    d_ker = d_ker.reshape(OWN, chips, pix_share, D).transpose(1, 0, 2, 3)
+    d_cols = scatter_z(d_ker, z).astype(bf16)
+    d_proj, d_cols = lax.optimization_barrier((d_proj, d_cols))
+    d_proj = scatter_z(d_proj, z)
+    d_cols_all = jnp.stack(in_order(terms(d_cols, "band", 1, BANDS), band), axis=0)
     d_cols_all = (
         d_cols_all.reshape(BANDS, SENSORS, SLOTS, pix_share * D)
         .transpose(1, 0, 2, 3)
         .reshape(SENSORS * BMAX, pix_share * D)
+        .astype(f32)
     )
     d_fc = xmm(h_all.reshape(SENSORS * BMAX, WG), d_cols_all, ((0,), (0,)))
-    dh = lax.psum(xmm(d_cols_all, fc_kernel, ((1,), (1,))), "tok")
+    dh = sum_tok(xmm(d_cols.reshape(OWN, pix_share * D).astype(f32), fc_kernel, ((1,), (1,))), chips)
+    dh = jnp.stack(in_order(terms(dh, "band", 1, BANDS), band)).reshape(BANDS, SENSORS, SLOTS, WG)
+    dh = dh.transpose(1, 0, 2, 3).reshape(SENSORS * BMAX, WG)
 
     block_sums = jnp.sum(de.reshape(CAP, CHIP, D).astype(f32), axis=1)
-    pick = (own_sensor[None, :] == sensor_ids[:, None]).astype(f32)
-    d_bias = jnp.sum(pick[:, :, None] * block_sums[None], axis=1)
+    which_sensor = (frame_sensor[0][None, :] == sensor_ids[:, None]).astype(f32)
+    d_bias = jnp.sum(which_sensor[:, :, None] * block_sums[None], axis=1)
     d_class = jnp.sum(tail_rows[:CAP], axis=0, keepdims=True)
-    smalls = lax.psum(
-        jnp.concatenate(
-            [d_bup[0].reshape(4, D), small1[0:1], small2[0:1], small1[1:2], small2[1:3], d_class, d_bias], axis=0
-        ),
-        BT,
-    )
+    smalls = jnp.concatenate(
+        [d_bup[0].reshape(4, D), small1[0:1], small2[0:1], small1[1:2], small2[1:3], d_class, d_bias], axis=0
+    )
+    smalls = tree_sum(terms(sum_tok(smalls, chips), "band", 1, BANDS))
     dbias_full = jnp.pad(smalls[10:17], ((0, 1), (0, 0)))
     g = gen_bwd(*gen_args, jnp.pad(dh, ((0, 4), (0, 0))), dbias_full)
-    bup_shard = lax.dynamic_slice_in_dim(smalls[0:4].reshape(FF), me * ff_share, ff_share, 0)
+    bup_shard = lax.dynamic_slice_in_dim(smalls[0:4], me * share, share, 1).reshape(ff_share)
     gains_shard = lax.dynamic_slice_in_dim(smalls[4:6], me * share, share, 1)
     shifts_shard = lax.dynamic_slice_in_dim(smalls[6:10], me * share, share, 1)
-    up_shard = ff_shard[: 4 * share].reshape(4, share, D).transpose(1, 0, 2).reshape(share, FF)
     return (
         out.reshape(1, 1, ROWS, D),
         d_pix.transpose(0, 2, 1).reshape(BANDS, 1, FRAME, width),
         tail_rows[CAP : 2 * CAP].reshape(1, 1, CAP, D),
-        proj_shard[:, : 3 * D],
-        proj_shard[:, 3 * D :],
-        up_shard,
+        d_proj[:, : 3 * D],
+        d_proj[:, 3 * D :],
+        d_ff[:, 0::2].reshape(share, 4, devices, share).transpose(0, 2, 1, 3).reshape(share, FF),
         bup_shard,
-        ff_shard[4 * share :],
+        d_ff[:, 1::2].transpose(1, 0, 2).reshape(ff_share, D),
         gains_shard,
         shifts_shard,
         g[0],

time: 835 us -> 582 us (0.70)
  waiting for transfers between devices: 415 us -> 197 us
  blocking collectives: 81.4 us -> 0 us
  starting transfers between devices: 5.35 us -> 48.5 us
  other arithmetic: 16.5 us -> 31.2 us
  local copies, waits for them, and re-layouts: 78 us -> 68.6 us
    ppermute x0 -> x46, waiting for transfers between devices: none -> 190 us  [flip(): lax.ppermute(v, axis, [(i, i ^ bits) for i in range(lax.axis_size(axis))])]
    all_gather x4 -> x1, waiting for transfers between devices: 197 us -> 7.5 us  [shards(): weights = lax.all_gather(weights, BT, axis=0, tiled=True)]
    reduce_scatter x2 -> x1, waiting for transfers between devices: 183 us -> 0.01 us  [shards(): lax.psum_scatter(d_ff, BT, scatter_dimension=0, tiled=True).astype(f32)]
    psum x2 -> x0, blocking collectives: 67.9 us -> none  [the longest x1 40.6 us: shards(): lax.psum(jnp.concatenate([d_bup[0].reshape(4, D), small1[0:1], small2[0:1...]
    ppermute x0 -> x46, starting transfers between devices: none -> 48 us  [flip(): lax.ppermute(v, axis, [(i, i ^ bits) for i in range(lax.axis_size(axis))])]
    unnamed x8 -> x2, waiting for transfers between devices: 35.2 us -> 0.03 us
    all_gather x1 -> x0, blocking collectives: 13.4 us -> none  [shards(): d_cols_all = lax.all_gather(d_cols, 'band', axis=0, tiled=False).astype(f32)]
    slice x10 -> x7, local copies, waits for them, and re-layouts: 18.7 us -> 8.1 us  [the longest x1 2.12 us: shards(): de_x[:half]]
  transfers between devices with their start and end apart: 8 -> 48, of which waited for: 6 -> 19; matrix products, arithmetic and copies ran while one was open for 8% -> 13% of each run, Pallas kernels for 9% -> 17%
where the time goes in v2:
time: 582 us; the launch traced here: 578 us
  Pallas kernels  209 us (36%)
  waiting for transfers between devices  197 us (34%)
  local copies, waits for them, and re-layouts  68.6 us (12%)
  starting transfers between devices  48.5 us (8%)
  other arithmetic  31.2 us (5%)
  between operations  15.4 us (3%)
  matrix products  8.43 us (1%)
    ppermute x46, waiting for transfers between devices, flip(): lax.ppermute(v, axis, [(i, i ^ bits) for i in range(lax.axis_size(axis))])  190 us
    pallas_call x1, Pallas kernels, attn_bwd(): pl.pallas_call(lambda *refs: attn_bwd_kernel(last, *refs), grid=(count,),...  64.4 us
    pallas_call x1, Pallas kernels, attn_fwd(): pl.pallas_call(attn_fwd_kernel, grid=(GROUPS,), in_specs=[whole((RP, D)),...  53.4 us
    ppermute x46, starting transfers between devices, flip(): lax.ppermute(v, axis, [(i, i ^ bits) for i in range(lax.axis_size(axis))])  48 us
    pallas_call x1, Pallas kernels, ffn(): pl.pallas_call(ffn_kernel, grid=(FF // FB,), in_specs=[whole((RP, D)), wh...  46.9 us
    pallas_call x3, Pallas kernels, pixel_grad(): pl.pallas_call(lambda *refs: pixel_grad_kernel(first, *refs), grid_spec=p...  17.1 us
    unnamed x130, local copies, waits for them, and re-layouts  16.8 us
    pallas_call x1, Pallas kernels, gen_bwd(): pl.pallas_call(gen_bwd_kernel, in_specs=[whole(a.shape) for a in args], o...  13.6 us
  transfers between devices with their start and end apart: 48, of which 19 were waited for; matrix products, arithmetic and copies ran while one was open for 13% of the time, Pallas kernels for 17%

profile of v2, /device:TPU:0, one launch (start us, length us, event | category | flops | bytes accessed | tf_op | source)
XLA Modules:
  0.0 578.1 jit_solution(7669315534395892570)
XLA Ops:
  7.3 2.1 reshape.320
  10.5 2.3 reshape.321
  21.9 4.6 gen_fwd.1
  28.4 3.8 fusion
  35.8 2.4 collective-permute-start.1
  38.2 1.5 collective-permute-start.2
  41.1 7.3 %collective-permute-done.1.refs_1_ = bf16[192,1024]{1,0:T(8,128)(2,1)S(1)} collective-permute-done((bf16[192,1024]{1,0:T(8,128)(2,1)}, bf16[192,1024]{1,0:T(8,128)(2,1)S(1)}, u32[]{:S(2)}, u32[]{:S(2)}) %collective-permute-start.1) | collective-permute-done | bytes 393248 | tf_op jit(solution)/shard_map/ppermute | solution.py:553
  48.4 8.9 %collective-permute-done.2.refs_2_ = bf16[192,1024]{1,0:T(8,128)(2,1)S(1)} collective-permute-done((bf16[192,1024]{1,0:T(8,128)(2,1)}, bf16[192,1024]{1,0:T(8,128)(2,1)S(1)}, u32[]{:S(2)}, u32[]{:S(2)}) %collective-permute-start.2) | collective-permute-done | bytes 393248 | tf_op jit(solution)/shard_map/ppermute | solution.py:553
  57.2 5.9 %collective-permute-done.3.refs_3_ = bf16[192,1024]{1,0:T(8,128)(2,1)S(1)} collective-permute-done((bf16[192,1024]{1,0:T(8,128)(2,1)}, bf16[192,1024]{1,0:T(8,128)(2,1)S(1)}, u32[]{:S(2)}, u32[]{:S(2)}) %collective-permute-start.3) | collective-permute-done | bytes 393248 | tf_op jit(solution)/shard_map/ppermute | solution.py:553
  63.1 1.9 maximum_select_fusion
  65.0 3.9 collective-permute-start.4
  70.4 11.0 %collective-permute-done.4 = bf16[21,16,384]{2,1,0:T(8,128)(2,1)} collective-permute-done((bf16[21,16,384]{2,1,0:T(8,128)(2,1)}, bf16[21,16,384]{2,1,0:T(8,128)(2,1)}, u32[]{:S(2)}, u32[]{:S(2)}) %collective-permute-start.4) | collective-permute-done | bytes 258080 | tf_op jit(solution)/shard_map/ppermute | solution.py:553
  81.3 18.0 %collective-permute-done.5 = bf16[21,16,384]{2,1,0:T(8,128)(2,1)} collective-permute-done((bf16[21,16,384]{2,1,0:T(8,128)(2,1)}, bf16[21,16,384]{2,1,0:T(8,128)(2,1)}, u32[]{:S(2)}, u32[]{:S(2)}) %collective-permute-start.5) | collective-permute-done | bytes 258080 | tf_op jit(solution)/shard_map/ppermute | solution.py:553
  99.4 1.8 broadcast_select_fusion.15
  101.3 1.8 collective-permute-start.7
  106.9 41.9 %collective-permute-done.7.refs_5_ = bf16[7,192,384]{2,1,0:T(8,128)(2,1)} collective-permute-done((bf16[7,192,384]{2,1,0:T(8,128)(2,1)S(1)}, bf16[7,192,384]{2,1,0:T(8,128)(2,1)}, u32[]{:S(2)}, u32[]{:S(2)}) %collective-permute-start.7) | collective-permute-done | bytes 1032224 | tf_op jit(solution)/shard_map/ppermute | solution.py:553
  149.4 22.1 %collective-permute-done.9.refs_7_ = bf16[7,192,384]{2,1,0:T(8,128)(2,1)} collective-permute-done((bf16[7,192,384]{2,1,0:T(8,128)(2,1)S(1)}, bf16[7,192,384]{2,1,0:T(8,128)(2,1)}, u32[]{:S(2)}, u32[]{:S(2)}) %collective-permute-start.9) | collective-permute-done | bytes 1032224 | tf_op jit(solution)/shard_map/ppermute | solution.py:553
  171.5 2.7 pad.28.dout
  174.7 7.5 %all-gather.2.cloned.1.call-done.wq.wk.wv.wo.wup.wdown.refs_1_.refs_7_.refs_8_.refs_9_ = bf16[768,9344]{1,0:T(8,128)(2,1)} async-done(((bf16[24,9344]{1,0:T(8,128)(2,1)}), bf16[768,9344]{1,0:T(8,128)(2,1)}) %all-gather.2.cloned.1.call-update) | async-done | bytes 14352400 | tf_op jit(solution)/shard_map/all_gather | solution.py:646
  182.2 1.6 slice.97
  187.8 8.4 %embed.1 = (f32[1040,768]{1,0:T(8,128)}, bf16[1040,768]{1,0:T(8,128)(2,1)S(1)}) custom-call(s32[4]{0:T(128)S(1)} %get-tuple-element.300.sens.refs_0_, s32[1]{0:T(128)} %bitcast.4.core.refs_2_, bf16[192,1024]{1,0:T(8,128)(2,1)S(1)} %get-tuple-element.72.refs_0_, bf16[192,1024]{1,0:T(8,128)(2,1)S(1)} %collective-permute-done.1.refs_1_, ...), custom_call_target="tpu_custom_call" | custom-call | flops 1207959552 | bytes 14680064 | tf_op jit(solution)/shard_map/embed/pallas_call | solution.py:233
  197.4 53.4 %attn_fwd.1 = (bf16[1040,768]{1,0:T(8,128)(2,1)}, bf16[1040,768]{1,0:T(8,128)(2,1)}, bf16[1040,768]{1,0:T(8,128)(2,1)}, bf16[1040,768]{1,0:T(8,128)(2,1)}, bf16[...) custom-call(bf16[1040,768]{1,0:T(8,128)(2,1)} %copy-done.35, ...), custom_call_target="tpu_custom_call" | custom-call | flops 49999998976 | bytes 52428800 | tf_op jit(solution)/shard_map/attn_fwd/pallas_call | solution.py:338
  250.8 46.9 %ffn.1 = (f32[1032,768]{1,0:T(8,128)}, bf16[768,6144]{1,0:T(8,128)(2,1)}, f32[8,3072]{1,0:T(8,128)}, f32[1040,768]{1,0:T(8,128)}, bf16[1040,768]{1,0:T(8,128)(2,1)}, /*index=5*/f32[8,768]{1,0:T(8,128)}) custom-call(bf16[1040,768]{1,0:T(8,128)(2,1)} %get-tuple-element.80.n2, bf16[1040,768]{1,0:T(8,128)(2,1)} %pad.28.dout, f32[1040,768]{1,0:T(8,128)} %get-tuple-element.81.x1, ...), custom_call_target="tpu_custom_call" | custom-call | flops 44999999488 | bytes 31457280 | tf_op jit(solution)/shard_map/ffn/pallas_call | solution.py:516
  297.7 1.9 broadcast_in_dim.67.refs_11_
  299.6 64.4 %attn_bwd.1 = (bf16[768,768]{1,0:T(8,128)(2,1)}, bf16[768,768]{1,0:T(8,128)(2,1)}, bf16[768,768]{1,0:T(8,128)(2,1)}, bf16[768,768]{1,0:T(8,128)(2,1)}, bf16[1024...) custom-call(bf16[1040,768]{1,0:T(8,128)(2,1)} %get-tuple-element.83.refs_0_, ...), custom_call_target="tpu_custom_call" | custom-call | flops 60000002048 | bytes 62914560 | tf_op jit(solution)/shard_map/attn_bwd/pallas_call | solution.py:434
  364.1 3.2 pad_maximum_fusion
  367.3 2.2 copy-done.36
  369.6 1.6 dynamic-slice_bitcast_fusion
  371.5 1.4 collective-permute-start.15
  375.3 1.6 convert_reduce_fusion
  377.0 4.9 fusion.1
  381.9 38.1 %collective-permute-done.15 = bf16[1024,768]{1,0:T(8,128)(2,1)} collective-permute-done((bf16[1024,768]{1,0:T(8,128)(2,1)}, bf16[1024,768]{1,0:T(8,128)(2,1)}, u32[]{:S(2)}, u32[]{:S(2)}) %collective-permute-start.15) | collective-permute-done | bytes 1572896 | tf_op jit(solution)/shard_map/ppermute | solution.py:553
  419.9 4.7 collective-permute-done.16
  424.6 2.1 slice.78
  427.3 2.1 slice.79
  432.7 5.0 pixel_grad.3
  437.8 2.9 collective-permute-start.31
  440.6 1.5 collective-permute-start.32
  442.1 2.2 pad_maximum_fusion.1.refs_3_
  444.3 7.5 %pixel_grad.4 = (f32[4,192,1024]{2,1,0:T(8,128)}, f32[7,192,768]{2,1,0:T(8,128)S(1)}) custom-call(s32[8]{0:T(128)S(1)} %pad_add_fusion.2.refs_0_, s32[2]{0:T(128)S(1)} %pad_add_fusion.3.refs_1_, s32[1]{0:T(128)} %bitcast.4.core.refs_2_, bf16[8,256,768]{2,1,0:T(8,128)(2,1)S(1)} %pad_maximum_fusion.1.refs_3_, ...), custom_call_target="tpu_custom_call", output_to_operand_aliasing={{0}: (7, {}), {1}: (8, {})} | custom-call | flops 1207959552 | bytes 8388608 | tf_op jit(solution)/shard_map/pixel_grad/pallas_call | solution.py:276
  451.8 1.5 pad_maximum_fusion.2
  453.3 4.6 pixel_grad.5
  460.7 1.4 collective-permute-start.33
  462.8 1.4 collective-permute-start.35
  465.3 2.0 collective-permute-done.34
  469.3 1.4 collective-permute-start.19
  471.4 1.4 collective-permute-start.21
  473.3 3.0 collective-permute-start.24
  476.4 9.2 %collective-permute-done.19 = bf16[4,24,3072]{2,1,0:T(8,128)(2,1)S(1)} collective-permute-done((bf16[4,24,3072]{2,1,0:T(8,128)(2,1)S(1)}, bf16[4,24,3072]{2,1,0:T(8,128)(2,1)S(1)}, u32[]{:S(2)}, u32[]{:S(2)}) %collective-permute-start.19) | collective-permute-done | bytes 589856 | tf_op jit(solution)/shard_map/ppermute | solution.py:553
  485.6 2.5 collective-permute-start.25
  488.1 8.5 %collective-permute-done.20 = bf16[4,24,3072]{2,1,0:T(8,128)(2,1)S(1)} collective-permute-done((bf16[4,24,3072]{2,1,0:T(8,128)(2,1)S(1)}, bf16[4,24,3072]{2,1,0:T(8,128)(2,1)S(1)}, u32[]{:S(2)}, u32[]{:S(2)}) %collective-permute-start.20) | collective-permute-done | bytes 589856 | tf_op jit(solution)/shard_map/ppermute | solution.py:553
  498.2 1.5 fusion.22
  500.9 3.7 collective-permute-start.38
  506.5 1.4 collective-permute-start.43
  510.9 1.8 collective-permute-start.40
  514.4 1.8 dynamic-slice_bitcast_fusion.14
  516.2 4.7 collective-permute-done.41
  522.0 2.1 collective-permute-start.28
  529.4 1.5 reshape.345
  531.8 13.6 %gen_bwd.1 = (f32[128,384]{1,0:T(8,128)}, f32[128,128]{1,0:T(8,128)}, f32[128,2048]{1,0:T(8,128)}, f32[2048,128]{1,0:T(8,128)}, f32[2,128]{1,0:T(2,128)}, /*inde...) custom-call(f32[96,128]{1,0:T(8,128)S(1)} %copy-done.16, f32[128,128]{1,0:T(8,128)S(1)} %copy-done.22, ...), custom_call_target="tpu_custom_call" | custom-call | tf_op jit(solution)/shard_map/gen_bwd/pallas_call | solution.py:195
  548.6 4.7 collective-permute-done.45
  557.6 3.1 fusion.23
  563.9 2.4 copy.172
  566.3 4.0 reshape.341
  (312 shorter events, 70.3 us)
Async XLA Ops:
  7.2 62.4 %copy-start = (s32[4,1,4]{2,1,0:T(1,128)S(1)}, s32[4,1,4]{2,1,0:T(1,128)}, u32[]{:S(2)}) copy-start(s32[4,1,4]{2,1,0:T(1,128)} %param.29) | copy-start | bytes 196
  7.2 175.0 %all-gather.2.cloned.1.call-start = ((), (), s32[]{:S(2)}) async-start(), calls=%async_computation.1 | async-start | bytes 14800896 | tf_op jit(solution)/shard_map/all_gather | solution.py:646
  18.5 542.2 %reduce-scatter.2.cloned.1.call-start = ((), (), s32[]{:S(2)}) async-start(), calls=%async_computation.2 | async-start | bytes 9732096 | tf_op jit(solution)/shard_map/reduce_scatter | solution.py:707
  34.3 6.8 %collective-permute-start = (bf16[21,8,384]{2,1,0:T(8,128)(2,1)}, bf16[21,8,384]{2,1,0:T(8,128)(2,1)}, u32[]{:S(2)}, u32[]{:S(2)}) collective-permute-start(bf16[21,8,384]{2,1,0:T(8,128)(2,1)} %bitcast.151), channel_id=1, source_target_pairs={{0,1},{1,0},{2,3},{3,2},{4,5},{5,4},{6,7},{7,6},{8,9},{9,8},{10,11... | collective-permute-start | bytes 387080 | tf_op jit(solution)/shard_map/ppermute | solution.py:553
  35.8 34.6 %copy-start.47 = (bf16[1,1,4,768]{3,2,1,0:T(4,128)(2,1)S(1)}, bf16[1,1,4,768]{3,2,1,0:T(4,128)(2,1)}, u32[]{:S(2)}) copy-start(bf16[1,1,4,768]{3,2,1,0:T(4,128)(2,1)} %param.31) | copy-start | bytes 18436
  35.8 12.6 %collective-permute-start.1 = (bf16[192,1024]{1,0:T(8,128)(2,1)}, bf16[192,1024]{1,0:T(8,128)(2,1)S(1)}, u32[]{:S(2)}, u32[]{:S(2)}) collective-permute-start(bf16[192,1024]{1,0:T(8,128)(2,1)} %get-tuple-element.267), channel_id=1, source_target_pairs={{0,8},{8,0},{16,24},{24,16},{1,9},{9,1},{17,25},{25,17},{2,10},{10... | collective-permute-start | bytes 1179656 | tf_op jit(solution)/shard_map/ppermute | solution.py:553
  38.2 19.0 %collective-permute-start.2 = (bf16[192,1024]{1,0:T(8,128)(2,1)}, bf16[192,1024]{1,0:T(8,128)(2,1)S(1)}, u32[]{:S(2)}, u32[]{:S(2)}) collective-permute-start(bf16[192,1024]{1,0:T(8,128)(2,1)} %get-tuple-element.266), channel_id=1, source_target_pairs={{0,16},{8,24},{16,0},{24,8},{1,17},{9,25},{17,1},{25,9},{2,18},{10... | collective-permute-start | bytes 1179656 | tf_op jit(solution)/shard_map/ppermute | solution.py:553
  39.7 23.4 %collective-permute-start.3 = (bf16[192,1024]{1,0:T(8,128)(2,1)}, bf16[192,1024]{1,0:T(8,128)(2,1)S(1)}, u32[]{:S(2)}, u32[]{:S(2)}) collective-permute-start(bf16[192,1024]{1,0:T(8,128)(2,1)} %get-tuple-element.265), channel_id=1, source_target_pairs={{0,24},{8,16},{16,8},{24,0},{1,25},{9,17},{17,9},{25,1},{2,26},{10... | collective-permute-start | bytes 1179656 | tf_op jit(solution)/shard_map/ppermute | solution.py:553
  57.2 43.9 %copy-start.17 = (bf16[192,1024]{1,0:T(8,128)(2,1)}, bf16[192,1024]{1,0:T(8,128)(2,1)S(1)}, u32[]{:S(2)}) copy-start(bf16[192,1024]{1,0:T(8,128)(2,1)S(1)} %collective-permute-done.2.refs_2_) | copy-start | bytes 1179652
  63.1 38.0 %copy-start.19 = (bf16[192,1024]{1,0:T(8,128)(2,1)}, bf16[192,1024]{1,0:T(8,128)(2,1)S(1)}, u32[]{:S(2)}) copy-start(bf16[192,1024]{1,0:T(8,128)(2,1)S(1)} %collective-permute-done.3.refs_3_) | copy-start | bytes 1179652
  65.0 16.3 %collective-permute-start.4 = (bf16[21,16,384]{2,1,0:T(8,128)(2,1)}, bf16[21,16,384]{2,1,0:T(8,128)(2,1)}, u32[]{:S(2)}, u32[]{:S(2)}) collective-permute-start(bf16[21,16,384]{2,1,0:T(8,128)(2,1)} %maximum_select_fusion), channel_id=1, source_target_pairs={{0,6},{1,7},{2,4},{3,5},{4,2},{5,3},{6,0},{7,1},{8,14},{9,15},{10,... | collective-permute-start | bytes 774152 | tf_op jit(solution)/shard_map/ppermute | solution.py:553
  69.0 30.4 %collective-permute-start.5 = (bf16[21,16,384]{2,1,0:T(8,128)(2,1)}, bf16[21,16,384]{2,1,0:T(8,128)(2,1)}, u32[]{:S(2)}, u32[]{:S(2)}) collective-permute-start(bf16[21,16,384]{2,1,0:T(8,128)(2,1)} %maximum_select_fusion), channel_id=1, source_target_pairs={{0,4},{1,5},{2,6},{3,7},{4,0},{5,1},{6,2},{7,3},{8,12},{9,13},{10,... | collective-permute-start | bytes 774152 | tf_op jit(solution)/shard_map/ppermute | solution.py:553
  69.0 30.4 %collective-permute-start.6 = (bf16[21,16,384]{2,1,0:T(8,128)(2,1)}, bf16[21,16,384]{2,1,0:T(8,128)(2,1)}, u32[]{:S(2)}, u32[]{:S(2)}) collective-permute-start(bf16[21,16,384]{2,1,0:T(8,128)(2,1)} %maximum_select_fusion), channel_id=1, source_target_pairs={{0,2},{1,3},{2,0},{3,1},{4,6},{5,7},{6,4},{7,5},{8,10},{9,11},{10,... | collective-permute-start | bytes 774152 | tf_op jit(solution)/shard_map/ppermute | solution.py:553
  101.3 84.4 %copy-start.2 = (bf16[21,64,384]{2,1,0:T(8,128)(2,1)}, bf16[21,64,384]{2,1,0:T(8,128)(2,1)S(1)}, u32[]{:S(2)}) copy-start(bf16[21,64,384]{2,1,0:T(8,128)(2,1)S(1)} %pad_maximum_fusion.3) | copy-start | bytes 3096580
  101.3 47.5 %collective-permute-start.7 = (bf16[7,192,384]{2,1,0:T(8,128)(2,1)S(1)}, bf16[7,192,384]{2,1,0:T(8,128)(2,1)}, u32[]{:S(2)}, u32[]{:S(2)}) collective-permute-start(bf16[7,192,384]{2,1,0:T(8,128)(2,1)S(1)} %bitcast.154), channel_id=1, source_target_pairs={{0,8},{8,0},{16,24},{24,16},{1,9},{9,1},{17,25},{25,17},{2,10},{10... | collective-permute-start | bytes 3096584 | tf_op jit(solution)/shard_map/ppermute | solution.py:553
  103.2 45.7 %collective-permute-start.8 = (bf16[7,192,384]{2,1,0:T(8,128)(2,1)S(1)}, bf16[7,192,384]{2,1,0:T(8,128)(2,1)}, u32[]{:S(2)}, u32[]{:S(2)}) collective-permute-start(bf16[7,192,384]{2,1,0:T(8,128)(2,1)S(1)} %bitcast.155), channel_id=1, source_target_pairs={{0,16},{8,24},{16,0},{24,8},{1,17},{9,25},{17,1},{25,9},{2,18},{10... | collective-permute-start | bytes 3096584 | tf_op jit(solution)/shard_map/ppermute | solution.py:553
  104.4 67.1 %collective-permute-start.9 = (bf16[7,192,384]{2,1,0:T(8,128)(2,1)S(1)}, bf16[7,192,384]{2,1,0:T(8,128)(2,1)}, u32[]{:S(2)}, u32[]{:S(2)}) collective-permute-start(bf16[7,192,384]{2,1,0:T(8,128)(2,1)S(1)} %bitcast.156), channel_id=1, source_target_pairs={{0,24},{8,16},{16,8},{24,0},{1,25},{9,17},{17,9},{25,1},{2,26},{10... | collective-permute-start | bytes 3096584 | tf_op jit(solution)/shard_map/ppermute | solution.py:553
  106.9 78.8 %collective-permute-start.10 = (bf16[7,192,384]{2,1,0:T(8,128)(2,1)S(1)}, bf16[7,192,384]{2,1,0:T(8,128)(2,1)}, u32[]{:S(2)}, u32[]{:S(2)}) collective-permute-start(bf16[7,192,384]{2,1,0:T(8,128)(2,1)S(1)} %bitcast.157), channel_id=1, source_target_pairs={{0,1},{1,0},{2,3},{3,2},{4,5},{5,4},{6,7},{7,6},{8,9},{9,8},{10,11... | collective-permute-start | bytes 3096584 | tf_op jit(solution)/shard_map/ppermute | solution.py:553
  148.8 36.9 %collective-permute-start.11 = (bf16[7,192,384]{2,1,0:T(8,128)(2,1)}, bf16[7,192,384]{2,1,0:T(8,128)(2,1)}, u32[]{:S(2)}, u32[]{:S(2)}) collective-permute-start(bf16[7,192,384]{2,1,0:T(8,128)(2,1)} %collective-permute-done.7.refs_5_), channel_id=1, source_target_pairs={{0,1},{1,0},{2,3},{3,2},{4,5},{5,4},{6,7},{7,6},{8,9},{9,8},{10,11... | collective-permute-start | bytes 3096584 | tf_op jit(solution)/shard_map/ppermute | solution.py:553
  148.9 36.9 %collective-permute-start.12 = (bf16[7,192,384]{2,1,0:T(8,128)(2,1)}, bf16[7,192,384]{2,1,0:T(8,128)(2,1)}, u32[]{:S(2)}, u32[]{:S(2)}) collective-permute-start(bf16[7,192,384]{2,1,0:T(8,128)(2,1)} %collective-permute-done.8.refs_6_), channel_id=1, source_target_pairs={{0,1},{1,0},{2,3},{3,2},{4,5},{5,4},{6,7},{7,6},{8,9},{9,8},{10,11... | collective-permute-start | bytes 3096584 | tf_op jit(solution)/shard_map/ppermute | solution.py:553
  171.5 14.3 %collective-permute-start.13 = (bf16[7,192,384]{2,1,0:T(8,128)(2,1)}, bf16[7,192,384]{2,1,0:T(8,128)(2,1)}, u32[]{:S(2)}, u32[]{:S(2)}) collective-permute-start(bf16[7,192,384]{2,1,0:T(8,128)(2,1)} %collective-permute-done.9.refs_7_), channel_id=1, source_target_pairs={{0,1},{1,0},{2,3},{3,2},{4,5},{5,4},{6,7},{7,6},{8,9},{9,8},{10,11... | collective-permute-start | bytes 3096584 | tf_op jit(solution)/shard_map/ppermute | solution.py:553
  371.2 5.8 collective-permute-start.14
  371.5 48.5 %collective-permute-start.15 = (bf16[1024,768]{1,0:T(8,128)(2,1)}, bf16[1024,768]{1,0:T(8,128)(2,1)}, u32[]{:S(2)}, u32[]{:S(2)}) collective-permute-start(bf16[1024,768]{1,0:T(8,128)(2,1)} %get-tuple-element.94), channel_id=1, source_target_pairs={{0,8},{8,0},{16,24},{24,16},{1,9},{9,1},{17,25},{25,17},{2,10},{10... | collective-permute-start | bytes 4718600 | tf_op jit(solution)/shard_map/ppermute | solution.py:553
  372.9 51.7 %collective-permute-start.16 = (bf16[1024,768]{1,0:T(8,128)(2,1)}, bf16[1024,768]{1,0:T(8,128)(2,1)}, u32[]{:S(2)}, u32[]{:S(2)}) collective-permute-start(bf16[1024,768]{1,0:T(8,128)(2,1)} %get-tuple-element.94), channel_id=1, source_target_pairs={{0,16},{8,24},{16,0},{24,8},{1,17},{9,25},{17,1},{25,9},{2,18},{10... | collective-permute-start | bytes 4718600 | tf_op jit(solution)/shard_map/ppermute | solution.py:553
  381.9 50.8 %copy-start.3 = (bf16[21,64,384]{2,1,0:T(8,128)(2,1)S(1)}, bf16[21,64,384]{2,1,0:T(8,128)(2,1)}, u32[]{:S(2)}) copy-start(bf16[21,64,384]{2,1,0:T(8,128)(2,1)} %copy-done.2) | copy-start | bytes 3096580
  426.7 25.1 %collective-permute-start.17 = (bf16[512,768]{1,0:T(8,128)(2,1)}, bf16[512,768]{1,0:T(8,128)(2,1)}, u32[]{:S(2)}, u32[]{:S(2)}) collective-permute-start(bf16[512,768]{1,0:T(8,128)(2,1)} %slice.78), channel_id=1, source_target_pairs={{0,16},{8,24},{16,0},{24,8},{1,17},{9,25},{17,1},{25,9},{2,18},{10... | collective-permute-start | bytes 2359304 | tf_op jit(solution)/shard_map/ppermute | solution.py:553
  429.4 22.5 %collective-permute-start.18 = (bf16[512,768]{1,0:T(8,128)(2,1)}, bf16[512,768]{1,0:T(8,128)(2,1)}, u32[]{:S(2)}, u32[]{:S(2)}) collective-permute-start(bf16[512,768]{1,0:T(8,128)(2,1)} %slice.79), channel_id=1, source_target_pairs={{0,8},{8,0},{16,24},{24,16},{1,9},{9,1},{17,25},{25,17},{2,10},{10... | collective-permute-start | bytes 2359304 | tf_op jit(solution)/shard_map/ppermute | solution.py:553
  432.6 5.1 collective-permute-start.29
  437.7 22.9 %collective-permute-start.30 = (f32[17,768]{1,0:T(8,128)S(1)}, f32[17,768]{1,0:T(8,128)S(1)}, u32[]{:S(2)}, u32[]{:S(2)}) collective-permute-start(f32[17,768]{1,0:T(8,128)S(1)} %add.197), channel_id=1, source_target_pairs={{0,2},{1,3},{2,0},{3,1},{4,6},{5,7},{6,4},{7,5},{8,10},{9,11},{10,... | collective-permute-start | bytes 156680 | tf_op jit(solution)/shard_map/ppermute | solution.py:553
  437.8 22.9 %collective-permute-start.31 = (f32[17,768]{1,0:T(8,128)S(1)}, f32[17,768]{1,0:T(8,128)S(1)}, u32[]{:S(2)}, u32[]{:S(2)}) collective-permute-start(f32[17,768]{1,0:T(8,128)S(1)} %add.197), channel_id=1, source_target_pairs={{0,4},{1,5},{2,6},{3,7},{4,0},{5,1},{6,2},{7,3},{8,12},{9,13},{10,... | collective-permute-start | bytes 156680 | tf_op jit(solution)/shard_map/ppermute | solution.py:553
  440.6 20.0 %collective-permute-start.32 = (f32[17,768]{1,0:T(8,128)S(1)}, f32[17,768]{1,0:T(8,128)S(1)}, u32[]{:S(2)}, u32[]{:S(2)}) collective-permute-start(f32[17,768]{1,0:T(8,128)S(1)} %add.197), channel_id=1, source_target_pairs={{0,6},{1,7},{2,4},{3,5},{4,2},{5,3},{6,0},{7,1},{8,14},{9,15},{10,... | collective-permute-start | bytes 156680 | tf_op jit(solution)/shard_map/ppermute | solution.py:553
  460.5 12.3 %collective-permute-start.22 = (bf16[1,84,8,768]{3,2,1,0:T(8,128)(2,1)}, bf16[1,84,8,768]{3,2,1,0:T(8,128)(2,1)S(1)}, u32[]{:S(2)}, u32[]{:S(2)}) collective-permute-start(bf16[1,84,8,768]{3,2,1,0:T(8,128)(2,1)} %dynamic-slice_bitcast_fusion.1), channel_id=1, source_target_pairs={{0,1},{1,0},{2,3},{3,2},{4,5},{5,4},{6,7},{7,6},{8,9},{9,8},{10,11... | collective-permute-start | bytes 3096584 | tf_op jit(solution)/shard_map/ppermute | solution.py:553
  460.7 4.6 collective-permute-start.33
  462.0 5.2 collective-permute-start.34
  462.8 5.4 collective-permute-start.35
  469.3 16.3 %collective-permute-start.19 = (bf16[4,24,3072]{2,1,0:T(8,128)(2,1)S(1)}, bf16[4,24,3072]{2,1,0:T(8,128)(2,1)S(1)}, u32[]{:S(2)}, u32[]{:S(2)}) collective-permute-start(bf16[4,24,3072]{2,1,0:T(8,128)(2,1)S(1)} %get-tuple-element.262), channel_id=1, source_target_pairs={{0,8},{8,0},{16,24},{24,16},{1,9},{9,1},{17,25},{25,17},{2,10},{10... | collective-permute-start | bytes 1769480 | tf_op jit(solution)/shard_map/ppermute | solution.py:553
  470.7 25.9 %collective-permute-start.20 = (bf16[4,24,3072]{2,1,0:T(8,128)(2,1)S(1)}, bf16[4,24,3072]{2,1,0:T(8,128)(2,1)S(1)}, u32[]{:S(2)}, u32[]{:S(2)}) collective-permute-start(bf16[4,24,3072]{2,1,0:T(8,128)(2,1)S(1)} %get-tuple-element.264), channel_id=1, source_target_pairs={{0,16},{8,24},{16,0},{24,8},{1,17},{9,25},{17,1},{25,9},{2,18},{10... | collective-permute-start | bytes 1769480 | tf_op jit(solution)/shard_map/ppermute | solution.py:553
  471.4 25.2 %collective-permute-start.21 = (bf16[4,24,3072]{2,1,0:T(8,128)(2,1)S(1)}, bf16[4,24,3072]{2,1,0:T(8,128)(2,1)S(1)}, u32[]{:S(2)}, u32[]{:S(2)}) collective-permute-start(bf16[4,24,3072]{2,1,0:T(8,128)(2,1)S(1)} %get-tuple-element.263), channel_id=1, source_target_pairs={{0,24},{8,16},{16,8},{24,0},{1,25},{9,17},{17,9},{25,1},{2,26},{10... | collective-permute-start | bytes 1769480 | tf_op jit(solution)/shard_map/ppermute | solution.py:553
  473.2 24.5 %collective-permute-start.23 = (bf16[21,8,768]{2,1,0:T(8,128)(2,1)S(1)}, bf16[21,8,768]{2,1,0:T(8,128)(2,1)S(1)}, u32[]{:S(2)}, u32[]{:S(2)}) collective-permute-start(bf16[21,8,768]{2,1,0:T(8,128)(2,1)S(1)} %get-tuple-element.273), channel_id=1, source_target_pairs={{0,2},{1,3},{2,0},{3,1},{4,6},{5,7},{6,4},{7,5},{8,10},{9,11},{10,... | collective-permute-start | bytes 774152 | tf_op jit(solution)/shard_map/ppermute | solution.py:553
  473.3 24.5 %collective-permute-start.24 = (bf16[21,8,768]{2,1,0:T(8,128)(2,1)S(1)}, bf16[21,8,768]{2,1,0:T(8,128)(2,1)S(1)}, u32[]{:S(2)}, u32[]{:S(2)}) collective-permute-start(bf16[21,8,768]{2,1,0:T(8,128)(2,1)S(1)} %get-tuple-element.275), channel_id=1, source_target_pairs={{0,4},{1,5},{2,6},{3,7},{4,0},{5,1},{6,2},{7,3},{8,12},{9,13},{10,... | collective-permute-start | bytes 774152 | tf_op jit(solution)/shard_map/ppermute | solution.py:553
  485.6 12.2 %collective-permute-start.25 = (bf16[21,8,768]{2,1,0:T(8,128)(2,1)S(1)}, bf16[21,8,768]{2,1,0:T(8,128)(2,1)S(1)}, u32[]{:S(2)}, u32[]{:S(2)}) collective-permute-start(bf16[21,8,768]{2,1,0:T(8,128)(2,1)S(1)} %get-tuple-element.274), channel_id=1, source_target_pairs={{0,6},{1,7},{2,4},{3,5},{4,2},{5,3},{6,0},{7,1},{8,14},{9,15},{10,... | collective-permute-start | bytes 774152 | tf_op jit(solution)/shard_map/ppermute | solution.py:553
  498.0 33.6 %copy-start.6 = (f32[128,2048]{1,0:T(8,128)S(1)}, f32[128,2048]{1,0:T(8,128)}, u32[]{:S(2)}) copy-start(f32[128,2048]{1,0:T(8,128)} %ff1.3) | copy-start | bytes 3145732
  498.1 33.6 %copy-start.8 = (f32[2048,128]{1,0:T(8,128)S(1)}, f32[2048,128]{1,0:T(8,128)}, u32[]{:S(2)}) copy-start(f32[2048,128]{1,0:T(8,128)} %ff2.3) | copy-start | bytes 3145732
  498.1 33.6 %copy-start.10 = (f32[128,768]{1,0:T(8,128)S(1)}, f32[128,768]{1,0:T(8,128)}, u32[]{:S(2)}) copy-start(f32[128,768]{1,0:T(8,128)} %fc_bias.3) | copy-start | bytes 1179652
  498.1 33.6 %copy-start.12 = (f32[96,224]{1,0:T(8,128)S(1)}, f32[96,224]{1,0:T(8,128)}, u32[]{:S(2)}) copy-start(f32[96,224]{1,0:T(8,128)} %copy-done.11) | copy-start | bytes 258052
  498.1 33.6 %copy-start.14 = (f32[128,384]{1,0:T(8,128)S(1)}, f32[128,384]{1,0:T(8,128)}, u32[]{:S(2)}) copy-start(f32[128,384]{1,0:T(8,128)} %w_qkv.3) | copy-start | bytes 589828
  498.1 33.6 %copy-start.16 = (f32[96,128]{1,0:T(8,128)S(1)}, f32[96,128]{1,0:T(8,128)}, u32[]{:S(2)}) copy-start(f32[96,128]{1,0:T(8,128)} %copy-done.15) | copy-start | bytes 147460
  498.1 33.6 %copy-start.22 = (f32[128,128]{1,0:T(8,128)S(1)}, f32[128,128]{1,0:T(8,128)}, u32[]{:S(2)}) copy-start(f32[128,128]{1,0:T(8,128)} %latent.3) | copy-start | bytes 196612
  498.1 33.6 %copy-start.24 = (f32[128,128]{1,0:T(8,128)S(1)}, f32[128,128]{1,0:T(8,128)}, u32[]{:S(2)}) copy-start(f32[128,128]{1,0:T(8,128)} %w_out.3) | copy-start | bytes 196612
  498.1 33.6 %copy-start.32 = (f32[2,128]{1,0:T(2,128)S(1)}, f32[2,128]{1,0:T(2,128)}, u32[]{:S(2)}) copy-start(f32[2,128]{1,0:T(2,128)} %gains.3) | copy-start | bytes 3076
  498.1 33.6 %copy-start.34 = (f32[2,128]{1,0:T(2,128)S(1)}, f32[2,128]{1,0:T(2,128)}, u32[]{:S(2)}) copy-start(f32[2,128]{1,0:T(2,128)} %shifts.3) | copy-start | bytes 3076
  499.7 1.2 collective-permute-start.36
  500.9 8.3 %collective-permute-start.37 = (f32[21,128]{1,0:T(8,128)S(1)}, f32[21,128]{1,0:T(8,128)S(1)}, u32[]{:S(2)}, u32[]{:S(2)}) collective-permute-start(f32[21,128]{1,0:T(8,128)S(1)} %add.206), channel_id=1, source_target_pairs={{0,2},{1,3},{2,0},{3,1},{4,6},{5,7},{6,4},{7,5},{8,10},{9,11},{10,... | collective-permute-start | bytes 32264 | tf_op jit(solution)/shard_map/ppermute | solution.py:553
  500.9 8.3 %collective-permute-start.38 = (f32[21,128]{1,0:T(8,128)S(1)}, f32[21,128]{1,0:T(8,128)S(1)}, u32[]{:S(2)}, u32[]{:S(2)}) collective-permute-start(f32[21,128]{1,0:T(8,128)S(1)} %add.206), channel_id=1, source_target_pairs={{0,4},{1,5},{2,6},{3,7},{4,0},{5,1},{6,2},{7,3},{8,12},{9,13},{10,... | collective-permute-start | bytes 32264 | tf_op jit(solution)/shard_map/ppermute | solution.py:553
  504.6 5.6 collective-permute-start.39
  506.5 42.1 %collective-permute-start.43 = (bf16[21,8,768]{2,1,0:T(8,128)(2,1)S(1)}, bf16[21,8,768]{2,1,0:T(8,128)(2,1)S(1)}, u32[]{:S(2)}, u32[]{:S(2)}) collective-permute-start(bf16[21,8,768]{2,1,0:T(8,128)(2,1)S(1)} %fusion.8), channel_id=1, source_target_pairs={{0,24},{8,16},{16,8},{24,0},{1,25},{9,17},{17,9},{25,1},{2,26},{10... | collective-permute-start | bytes 774152 | tf_op jit(solution)/shard_map/ppermute | solution.py:553
  508.0 40.7 %collective-permute-start.44 = (bf16[21,8,768]{2,1,0:T(8,128)(2,1)S(1)}, bf16[21,8,768]{2,1,0:T(8,128)(2,1)}, u32[]{:S(2)}, u32[]{:S(2)}) collective-permute-start(bf16[21,8,768]{2,1,0:T(8,128)(2,1)S(1)} %fusion.8), channel_id=1, source_target_pairs={{0,16},{8,24},{16,0},{24,8},{1,17},{9,25},{17,1},{25,9},{2,18},{10... | collective-permute-start | bytes 774152 | tf_op jit(solution)/shard_map/ppermute | solution.py:553
  510.9 5.3 collective-permute-start.40
  512.7 8.2 %collective-permute-start.41 = (f32[21,128]{1,0:T(8,128)S(1)}, f32[21,128]{1,0:T(8,128)S(1)}, u32[]{:S(2)}, u32[]{:S(2)}) collective-permute-start(f32[21,128]{1,0:T(8,128)S(1)} %add_add_fusion.2), channel_id=1, source_target_pairs={{0,16},{8,24},{16,0},{24,8},{1,17},{9,25},{17,1},{25,9},{2,18},{10... | collective-permute-start | bytes 32264 | tf_op jit(solution)/shard_map/ppermute | solution.py:553
  513.0 8.9 %collective-permute-start.42 = (f32[21,128]{1,0:T(8,128)S(1)}, f32[21,128]{1,0:T(8,128)S(1)}, u32[]{:S(2)}, u32[]{:S(2)}) collective-permute-start(f32[21,128]{1,0:T(8,128)S(1)} %add_add_fusion.2), channel_id=1, source_target_pairs={{0,8},{8,0},{16,24},{24,16},{1,9},{9,1},{17,25},{25,17},{2,10},{10... | collective-permute-start | bytes 32264 | tf_op jit(solution)/shard_map/ppermute | solution.py:553
  516.2 29.2 %collective-permute-start.26 = (bf16[24,3072]{1,0:T(8,128)(2,1)}, bf16[24,3072]{1,0:T(8,128)(2,1)}, u32[]{:S(2)}, u32[]{:S(2)}) collective-permute-start(bf16[24,3072]{1,0:T(8,128)(2,1)} %get-tuple-element.280), channel_id=1, source_target_pairs={{0,2},{1,3},{2,0},{3,1},{4,6},{5,7},{6,4},{7,5},{8,10},{9,11},{10,... | collective-permute-start | bytes 442376 | tf_op jit(solution)/shard_map/ppermute | solution.py:553
  520.9 25.1 %collective-permute-start.27 = (bf16[24,3072]{1,0:T(8,128)(2,1)}, bf16[24,3072]{1,0:T(8,128)(2,1)}, u32[]{:S(2)}, u32[]{:S(2)}) collective-permute-start(bf16[24,3072]{1,0:T(8,128)(2,1)} %get-tuple-element.282), channel_id=1, source_target_pairs={{0,4},{1,5},{2,6},{3,7},{4,0},{5,1},{6,2},{7,3},{8,12},{9,13},{10,... | collective-permute-start | bytes 442376 | tf_op jit(solution)/shard_map/ppermute | solution.py:553
  522.0 24.1 %collective-permute-start.28 = (bf16[24,3072]{1,0:T(8,128)(2,1)}, bf16[24,3072]{1,0:T(8,128)(2,1)}, u32[]{:S(2)}, u32[]{:S(2)}) collective-permute-start(bf16[24,3072]{1,0:T(8,128)(2,1)} %get-tuple-element.281), channel_id=1, source_target_pairs={{0,6},{1,7},{2,4},{3,5},{4,2},{5,3},{6,0},{7,1},{8,14},{9,15},{10,... | collective-permute-start | bytes 442376 | tf_op jit(solution)/shard_map/ppermute | solution.py:553
  545.4 7.9 %collective-permute-start.45 = (bf16[21,8,768]{2,1,0:T(8,128)(2,1)S(1)}, bf16[21,8,768]{2,1,0:T(8,128)(2,1)S(1)}, u32[]{:S(2)}, u32[]{:S(2)}) collective-permute-start(bf16[21,8,768]{2,1,0:T(8,128)(2,1)S(1)} %fusion.8), channel_id=1, source_target_pairs={{0,8},{8,0},{16,24},{24,16},{1,9},{9,1},{17,25},{25,17},{2,10},{10... | collective-permute-start | bytes 774152 | tf_op jit(solution)/shard_map/ppermute | solution.py:553
  (41 other events, 288.4 us)
Sparse Core Ops, SparseCore 0:
  18.7 163.5 all-gather.1
  297.8 155.2 reduce-scatter.1
